TPU v7x, 32 devices: a whole 2x2x4 slice. The times are simulated.
32 devices in a mesh: dp: 4 (over y, x), row: 2 (over core), col: 4 (over z).
Axes of the slice: x: 2, y: 2, z: 4, core: 2. Of those that a mesh axis runs over, the one named last changes fastest.
Arguments:
- pixels: bfloat16 [4, 64, 384, 256], P('dp', 'row', 'col'), may hold values from -6 to 6
- hidden_pre: bfloat16 [4, 32, 192, 256], P('dp', 'row', 'col'), may hold values from -6 to 6
- upstream: bfloat16 [4, 16, 96, 512], P('dp', 'row', 'col'), may hold values from -6 to 6
- kernel_first: bfloat16 [3, 3, 256, 256], replicated, may hold values from -0.125 to 0.125
- kernel_second: bfloat16 [3, 3, 256, 512], replicated, may hold values from -0.125 to 0.125
Outputs:
- grad_pixels: bfloat16 [4, 64, 384, 256], P('dp', 'row', 'col')
- grad_kernel_first: float32 [2304, 256], P(('row', 'col'))
- grad_kernel_second: float32 [2304, 512], P(('row', 'col'))
All inputs are finite; a program needn't handle non-finite values.
Results may differ from a plain program's by a relative error of at most 0.0049.
Values may be sent and summed in bfloat16 or wider, within the bound.
A program may use at most 64 MiB of HBM per device.

v0:
```python
import math

import jax
import jax.numpy as jnp
from jax import lax
from jax.sharding import PartitionSpec as P


def shifted(value, axis, by):
    peers = lax.axis_size(axis)
    pairs = [(i, i + by) for i in range(peers) if 0 <= i + by < peers]
    return lax.ppermute(value, axis, pairs)


def extend_field(tile_field):
    from_above = shifted(tile_field[-1], "row", 1)
    from_left = shifted(tile_field[:, -1], "col", 1)
    corner = shifted(from_left[-1:], "row", 1)
    top_row = jnp.concatenate([corner, from_above], axis=0)
    lower_rows = jnp.concatenate([from_left[:, None], tile_field], axis=1)
    return jnp.concatenate([top_row[None], lower_rows], axis=0)


def gather_taps(extended, out_rows, out_cols):
    tap_list = []
    for tap_row in range(3):
        for tap_col in range(3):
            tap_list.append(
                extended[tap_row : tap_row + 2 * out_rows : 2, tap_col : tap_col + 2 * out_cols : 2]
            )
    stacked = jnp.concatenate(tap_list, axis=-1)
    return stacked.reshape(out_rows * out_cols, stacked.shape[-1])


def spread_taps(tap_terms):
    row_count = tap_terms.shape[0]
    col_count = tap_terms.shape[1]
    channels = tap_terms.shape[-1]
    even_part = jnp.pad(tap_terms[:, :, 0], ((0, 1), (0, 0), (0, 0), (0, 0))) + jnp.pad(
        tap_terms[:, :, 2], ((1, 0), (0, 0), (0, 0), (0, 0))
    )
    odd_part = jnp.pad(tap_terms[:, :, 1], ((0, 1), (0, 0), (0, 0), (0, 0)))
    merged = jnp.stack([even_part, odd_part], axis=1).reshape(
        2 * row_count + 2, col_count, 3, channels
    )[: 2 * row_count + 1]
    even_part = jnp.pad(merged[:, :, 0], ((0, 0), (0, 1), (0, 0))) + jnp.pad(
        merged[:, :, 2], ((0, 0), (1, 0), (0, 0))
    )
    odd_part = jnp.pad(merged[:, :, 1], ((0, 0), (0, 1), (0, 0)))
    return jnp.stack([even_part, odd_part], axis=2).reshape(
        2 * row_count + 1, 2 * col_count + 2, channels
    )[:, : 2 * col_count + 1]


def settle_edges(padded):
    interior = padded[1:, 1:]
    from_below = shifted(padded[0, 1:], "row", -1)
    from_right = shifted(padded[:, 0], "col", -1)
    corner = shifted(from_right[:1], "row", -1)
    from_below = from_below.at[-1].add(corner[0])
    interior = interior.at[:, -1].add(from_right[1:])
    return interior.at[-1].add(from_below)


def kernel_gradient(patches, gradient, norm_scale):
    slide_sums = lax.psum(
        lax.dot_general(
            patches, gradient, (((0,), (0,)), ((), ())), preferred_element_type=jnp.float32
        )
        * norm_scale,
        "dp",
    )
    return lax.psum_scatter(slide_sums, ("row", "col"), scatter_dimension=0, tiled=True)


def per_device(pixels, hidden_pre, upstream, kernel_first, kernel_second):
    source = pixels[0]
    hidden = hidden_pre[0]
    cotangent_tile = upstream[0]
    rows_two, cols_two, width_two = cotangent_tile.shape
    rows_one, cols_one, width_one = hidden.shape
    width_zero = source.shape[-1]
    devices_all = lax.axis_size("dp") * lax.axis_size("row") * lax.axis_size("col")
    scale_one = 1.0 / math.sqrt(devices_all * rows_one * cols_one)
    scale_two = 1.0 / math.sqrt(devices_all * rows_two * cols_two)
    flat_second = kernel_second.reshape(9 * width_one, width_two)
    flat_first = kernel_first.reshape(9 * width_zero, width_one)
    cotangent = cotangent_tile.reshape(rows_two * cols_two, width_two)
    terms_two = lax.dot_general(
        cotangent, flat_second, (((1,), (1,)), ((), ())), preferred_element_type=jnp.float32
    )
    grad_active = settle_edges(spread_taps(terms_two.reshape(rows_two, cols_two, 3, 3, width_one)))
    active = jnp.maximum(hidden, 0)
    active_patches = gather_taps(extend_field(active), rows_two, cols_two)
    grad_kernel_second = kernel_gradient(active_patches, cotangent, scale_two)
    grad_pre = jnp.where(hidden > 0, grad_active, 0.0).astype(jnp.bfloat16)
    grad_rows = grad_pre.reshape(rows_one * cols_one, width_one)
    terms_one = lax.dot_general(
        grad_rows, flat_first, (((1,), (1,)), ((), ())), preferred_element_type=jnp.float32
    )
    grad_source = settle_edges(
        spread_taps(terms_one.reshape(rows_one, cols_one, 3, 3, width_zero))
    ).astype(jnp.bfloat16)
    source_patches = gather_taps(extend_field(source), rows_one, cols_one)
    grad_kernel_first = kernel_gradient(source_patches, grad_rows, scale_one)
    return (grad_source[None], grad_kernel_first, grad_kernel_second)


def solution(mesh):
    in_specs = (
        P("dp", "row", "col", None),
        P("dp", "row", "col", None),
        P("dp", "row", "col", None),
        P(),
        P(),
    )
    out_specs = (P("dp", "row", "col", None), P(("row", "col"), None), P(("row", "col"), None))
    return jax.shard_map(
        per_device, mesh=mesh, in_specs=in_specs, out_specs=out_specs, check_vma=False
    )
```

profile of v0, /device:TPU:0, one launch (start us, length us, event | category | flops | bytes accessed | tf_op | source)
XLA Modules:
  0.0 331.8 jit_solution(14036254897099947175)
XLA Ops:
  7.2 1.6 copy-done
  8.8 1.8 fusion.1
  11.6 1.6 copy.44
  13.2 1.8 reshape.226
  15.6 1.3 collective-permute-start
  16.9 0.6 slice_bitcast_fusion.13
  17.5 1.3 collective-permute-start.1
  19.5 6.1 %collective-permute-start.6 = (bf16[32,256]{1,0:T(8,128)(2,1)}, bf16[32,256]{1,0:T(8,128)(2,1)}, u32[]{:S(2)}, u32[]{:S(2)}) collective-permute-start(bf16[32,256]{1,0:T(8,128)(2,1)} %bitcast.134), channel_id=1, source_target_pairs={{0,1},{1,2},{2,3},{4,5},{5,6},{6,7},{8,9},{9,10},{10,11},{12,13},{... | collective-permute-start | bytes 49160 | tf_op jit(solution)/shard_map/ppermute | solution.py:12
  26.2 4.0 %collective-permute-start.8 = (bf16[96,256]{1,0:T(8,128)(2,1)}, bf16[96,256]{1,0:T(8,128)(2,1)}, u32[]{:S(2)}, u32[]{:S(2)}) collective-permute-start(bf16[96,256]{1,0:T(8,128)(2,1)} %slice_bitcast_fusion.14), channel_id=1, source_target_pairs={{0,4},{1,5},{2,6},{3,7},{8,12},{9,13},{10,14},{11,15},{16,20},{17,... | collective-permute-start | bytes 147464 | tf_op jit(solution)/shard_map/ppermute | solution.py:12
  30.3 5.1 %slice.315 = bf16[16,48,256]{2,1,0:T(8,128)(2,1)} slice(bf16[32,96,256]{2,1,0:T(8,128)(2,1)S(1)} %bitcast.138), slice={[0:32:2], [0:96:2], [0:256:1]} | slice | bytes 786432 | tf_op jit(solution)/shard_map/slice | solution.py:29
  35.4 0.7 slice.316
  36.1 1.0 slice.318
  37.2 1.0 slice.319
  38.2 0.7 copy.58
  39.6 2.1 pad_maximum_fusion.2
  41.7 9.2 %slice.314 = bf16[16,48,256]{2,1,0:T(8,128)(2,1)} slice(bf16[32,97,256]{2,1,0:T(8,128)(2,1)} %pad_maximum_fusion.2), slice={[0:32:2], [0:96:2], [0:256:1]} | slice | bytes 786432 | tf_op jit(solution)/shard_map/slice | solution.py:29
  50.9 9.1 %slice.317 = bf16[16,48,256]{2,1,0:T(8,128)(2,1)} slice(bf16[32,97,256]{2,1,0:T(8,128)(2,1)} %pad_maximum_fusion.2), slice={[1:32:2], [0:96:2], [0:256:1]} | slice | bytes 786432 | tf_op jit(solution)/shard_map/slice | solution.py:29
  60.0 1.3 slice.361
  61.2 1.8 collective-permute-start.7
  63.1 0.7 fusion.10
  63.8 1.3 slice.345
  65.1 1.3 collective-permute-start.2
  66.5 0.8 maximum_bitcast_fusion
  67.3 3.0 maximum_maximum_fusion
  70.4 7.6 %slice.311 = bf16[16,48,256]{2,1,0:T(8,128)(2,1)S(1)} slice(bf16[33,97,256]{2,1,0:T(8,128)(2,1)} %maximum_maximum_fusion), slice={[0:32:2], [0:96:2], [0:256:1]} | slice | bytes 786432 | tf_op jit(solution)/shard_map/slice | solution.py:29
  78.0 0.8 constant_dynamic-update-slice_fusion.8
  78.8 9.2 %slice.312 = bf16[16,48,256]{2,1,0:T(8,128)(2,1)} slice(bf16[33,97,256]{2,1,0:T(8,128)(2,1)} %maximum_maximum_fusion), slice={[0:32:2], [1:97:2], [0:256:1]} | slice | bytes 786432 | tf_op jit(solution)/shard_map/slice | solution.py:29
  88.0 7.6 %slice.313 = bf16[16,48,256]{2,1,0:T(8,128)(2,1)S(1)} slice(bf16[33,97,256]{2,1,0:T(8,128)(2,1)} %maximum_maximum_fusion), slice={[0:32:2], [2:97:2], [0:256:1]} | slice | bytes 786432 | tf_op jit(solution)/shard_map/slice | solution.py:29
  95.6 0.7 fusion.12
  96.4 1.3 scatter-add.21
  97.7 0.8 fusion.8
  98.5 1.8 constant_dynamic-update-slice_fusion.7
  100.3 0.8 constant_dynamic-update-slice_fusion.6
  101.1 0.8 constant_dynamic-update-slice_fusion.5
  101.9 0.9 constant_dynamic-update-slice_fusion.4
  102.7 0.8 constant_dynamic-update-slice_fusion.3
  103.6 0.8 constant_dynamic-update-slice_fusion.2
  104.4 0.8 constant_dynamic-update-slice_fusion.1
  105.2 0.8 constant_dynamic-update-slice_fusion
  106.0 4.6 %fusion = f32[2304,256]{1,0:T(8,128)} fusion(bf16[16,48,2304]{2,1,0:T(8,128)(2,1)} %constant_dynamic-update-slice_fusion, f32[16,48,256]{2,1,0:T(8,128)S(1)} %fusion.8, bf16[1,16,48,256]{3,2,1,0:T(8,128)(2,1)S(1)} %copy-done.3), kind=kOutput, calls=%fused_computation.3 | convolution fusion | flops 907345920 | bytes 7077888 | tf_op jit(solution)/shard_map/dot_general | solution.py:67
  110.8 3.3 %collective-permute-start.9 = (bf16[16,256]{1,0:T(8,128)(2,1)S(1)}, bf16[16,256]{1,0:T(8,128)(2,1)S(1)}, u32[]{:S(2)}, u32[]{:S(2)}) collective-permute-start(bf16[16,256]{1,0:T(8,128)(2,1)S(1)} %bitcast.150), channel_id=1, source_target_pairs={{0,1},{1,2},{2,3},{4,5},{5,6},{6,7},{8,9},{9,10},{10,11},{12,13},{... | collective-permute-start | bytes 24584 | tf_op jit(solution)/shard_map/ppermute | solution.py:12
  114.2 3.3 collective-permute-start.11
  119.0 1.3 collective-permute-start.10
  122.4 3.0 convolution_multiply_fusion
  125.6 1.0 copy-done.7
  126.7 1.1 fusion.3
  127.8 0.7 slice_bitcast_fusion.2
  131.3 3.4 %copy.53 = f32[33,49,2,256]{3,2,1,0:T(2,128)} copy(f32[33,49,2,256]{3,1,0,2:T(8,128)S(1)} %pad_maximum_fusion.1) | data formatting | bytes 6623232 | tf_op jit(solution)/shard_map/stack | solution.py:50
  134.7 4.0 %reshape.231 = f32[33,98,256]{2,1,0:T(8,128)S(1)} reshape(f32[33,49,2,256]{3,2,1,0:T(2,128)} %copy.53) | data formatting | bytes 6623232 | tf_op jit(solution)/shard_map/reshape | solution.py:50
  138.8 1.3 collective-permute-start.3
  140.1 0.7 slice_bitcast_fusion.12
  140.8 2.1 slice.352
  142.9 1.3 collective-permute-start.4
  144.2 2.7 collective-permute-done.3
  147.6 1.3 collective-permute-start.5
  148.8 18.9 %reduce-scatter.3.cloned.1.call-done = f32[288,256]{1,0:T(8,128)} async-done(((f32[2304,256]{1,0:T(8,128)}), f32[288,256]{1,0:T(8,128)}) %reduce-scatter.3.cloned.1.call-update) | async-done | bytes 294928 | tf_op jit(solution)/shard_map/reduce_scatter | solution.py:73
  167.7 100.3 %reduce-scatter.5.cloned.1.call-done = f32[288,512]{1,0:T(8,128)} async-done(((f32[2304,512]{1,0:T(8,128)}), f32[288,512]{1,0:T(8,128)}) %reduce-scatter.5.cloned.1.call-update) | async-done | bytes 589840 | tf_op jit(solution)/shard_map/reduce_scatter | solution.py:73
  268.1 0.8 fusion.9
  268.9 1.8 scatter-add.25
  270.7 1.7 fusion.7
  272.4 3.3 convert_bitcast_fusion
  275.7 45.9 %all-reduce.15.cloned.1.call-done = (f32[288,256]{1,0:T(8,128)}, f32[288,512]{1,0:T(8,128)}) async-done(((f32[288,256]{1,0:T(8,128)}, f32[288,512]{1,0:T(8,128)}), (f32[288,256]{1,0:T(8,128)}, f32[288,512]{1,0:T(8,128)})) %all-reduce.15.cloned.1.call-update) | async-done | bytes 884752 | tf_op jit(solution)/shard_map/psum | solution.py:66
  321.6 1.7 copy.111
  323.3 1.9 copy.112
  (96 shorter events, 11.0 us)
Async XLA Ops:
  7.2 1.7 copy-start
  7.2 160.6 %reduce-scatter.3.cloned.1.call-start = ((), (), s32[]{:S(2)}) async-start(), calls=%async_computation.2 | async-start | bytes 2654208 | tf_op jit(solution)/shard_map/reduce_scatter | solution.py:73
  11.6 7.2 %copy-start.2 = (bf16[1,32,96,256]{3,2,1,0:T(8,128)(2,1)S(1)}, bf16[1,32,96,256]{3,2,1,0:T(8,128)(2,1)}, u32[]{:S(2)}) copy-start(bf16[1,32,96,256]{3,2,1,0:T(8,128)(2,1)} %param.17) | copy-start | bytes 4718596
  15.6 47.5 %collective-permute-start = (f32[17,256]{1,0:T(8,128)}, f32[17,256]{1,0:T(8,128)}, u32[]{:S(2)}, u32[]{:S(2)}) collective-permute-start(f32[17,256]{1,0:T(8,128)} %bitcast.133), channel_id=1, source_target_pairs={{1,0},{2,1},{3,2},{5,4},{6,5},{7,6},{9,8},{10,9},{11,10},{13,12},{... | collective-permute-start | bytes 52232 | tf_op jit(solution)/shard_map/ppermute | solution.py:12
  17.5 78.1 %collective-permute-start.1 = (f32[48,256]{1,0:T(8,128)}, f32[48,256]{1,0:T(8,128)}, u32[]{:S(2)}, u32[]{:S(2)}) collective-permute-start(f32[48,256]{1,0:T(8,128)} %slice_bitcast_fusion.13), channel_id=1, source_target_pairs={{4,0},{5,1},{6,2},{7,3},{12,8},{13,9},{14,10},{15,11},{20,16},{21,... | collective-permute-start | bytes 147464 | tf_op jit(solution)/shard_map/ppermute | solution.py:12
  19.5 18.7 %collective-permute-start.6 = (bf16[32,256]{1,0:T(8,128)(2,1)}, bf16[32,256]{1,0:T(8,128)(2,1)}, u32[]{:S(2)}, u32[]{:S(2)}) collective-permute-start(bf16[32,256]{1,0:T(8,128)(2,1)} %bitcast.134), channel_id=1, source_target_pairs={{0,1},{1,2},{2,3},{4,5},{5,6},{6,7},{8,9},{9,10},{10,11},{12,13},{... | collective-permute-start | bytes 49160 | tf_op jit(solution)/shard_map/ppermute | solution.py:12
  26.2 40.3 %collective-permute-start.8 = (bf16[96,256]{1,0:T(8,128)(2,1)}, bf16[96,256]{1,0:T(8,128)(2,1)}, u32[]{:S(2)}, u32[]{:S(2)}) collective-permute-start(bf16[96,256]{1,0:T(8,128)(2,1)} %slice_bitcast_fusion.14), channel_id=1, source_target_pairs={{0,4},{1,5},{2,6},{3,7},{8,12},{9,13},{10,14},{11,15},{16,20},{17,... | collective-permute-start | bytes 147464 | tf_op jit(solution)/shard_map/ppermute | solution.py:12
  39.0 0.6 copy-start.8
  61.2 5.3 %collective-permute-start.7 = (bf16[1,256]{1,0:T(2,128)(2,1)}, bf16[1,256]{1,0:T(2,128)(2,1)}, u32[]{:S(2)}, u32[]{:S(2)}) collective-permute-start(bf16[1,256]{1,0:T(2,128)(2,1)} %slice.361), channel_id=1, source_target_pairs={{0,4},{1,5},{2,6},{3,7},{8,12},{9,13},{10,14},{11,15},{16,20},{17,... | collective-permute-start | bytes 1544 | tf_op jit(solution)/shard_map/ppermute | solution.py:12
  65.1 30.5 %collective-permute-start.2 = (f32[1,256]{1,0:T(1,128)}, f32[1,256]{1,0:T(1,128)}, u32[]{:S(2)}, u32[]{:S(2)}) collective-permute-start(f32[1,256]{1,0:T(1,128)} %slice.345), channel_id=1, source_target_pairs={{4,0},{5,1},{6,2},{7,3},{12,8},{13,9},{14,10},{15,11},{20,16},{21,... | collective-permute-start | bytes 3080 | tf_op jit(solution)/shard_map/ppermute | solution.py:12
  70.4 30.7 %copy-start.6 = (bf16[16,48,256]{2,1,0:T(8,128)(2,1)S(1)}, bf16[16,48,256]{2,1,0:T(8,128)(2,1)}, u32[]{:S(2)}) copy-start(bf16[16,48,256]{2,1,0:T(8,128)(2,1)} %slice.314) | copy-start | bytes 1179652
  78.0 23.9 %copy-start.4 = (bf16[16,48,256]{2,1,0:T(8,128)(2,1)S(1)}, bf16[16,48,256]{2,1,0:T(8,128)(2,1)}, u32[]{:S(2)}) copy-start(bf16[16,48,256]{2,1,0:T(8,128)(2,1)} %slice.315) | copy-start | bytes 1179652
  88.0 15.6 %copy-start.5 = (bf16[16,48,256]{2,1,0:T(8,128)(2,1)S(1)}, bf16[16,48,256]{2,1,0:T(8,128)(2,1)}, u32[]{:S(2)}) copy-start(bf16[16,48,256]{2,1,0:T(8,128)(2,1)} %slice.317) | copy-start | bytes 1179652
  101.1 5.0 %copy-start.3 = (bf16[1,16,48,256]{3,2,1,0:T(8,128)(2,1)S(1)}, bf16[1,16,48,256]{3,2,1,0:T(8,128)(2,1)}, u32[]{:S(2)}) copy-start(bf16[1,16,48,256]{3,2,1,0:T(8,128)(2,1)} %param.18) | copy-start | bytes 1179652
  110.7 157.4 %reduce-scatter.5.cloned.1.call-start = ((), (), s32[]{:S(2)}) async-start(), calls=%async_computation.3 | async-start | bytes 5308416 | tf_op jit(solution)/shard_map/reduce_scatter | solution.py:73
  110.8 8.2 %collective-permute-start.9 = (bf16[16,256]{1,0:T(8,128)(2,1)S(1)}, bf16[16,256]{1,0:T(8,128)(2,1)S(1)}, u32[]{:S(2)}, u32[]{:S(2)}) collective-permute-start(bf16[16,256]{1,0:T(8,128)(2,1)S(1)} %bitcast.150), channel_id=1, source_target_pairs={{0,1},{1,2},{2,3},{4,5},{5,6},{6,7},{8,9},{9,10},{10,11},{12,13},{... | collective-permute-start | bytes 24584 | tf_op jit(solution)/shard_map/ppermute | solution.py:12
  114.2 7.0 %collective-permute-start.11 = (bf16[48,256]{1,0:T(8,128)(2,1)S(1)}, bf16[48,256]{1,0:T(8,128)(2,1)S(1)}, u32[]{:S(2)}, u32[]{:S(2)}) collective-permute-start(bf16[48,256]{1,0:T(8,128)(2,1)S(1)} %slice_bitcast_fusion.16), channel_id=1, source_target_pairs={{0,4},{1,5},{2,6},{3,7},{8,12},{9,13},{10,14},{11,15},{16,20},{17,... | collective-permute-start | bytes 73736 | tf_op jit(solution)/shard_map/ppermute | solution.py:12
  118.1 4.3 %copy-start.9 = (bf16[1,8,24,512]{3,2,1,0:T(8,128)(2,1)S(1)}, bf16[1,8,24,512]{3,2,1,0:T(8,128)(2,1)}, u32[]{:S(2)}) copy-start(bf16[1,8,24,512]{3,2,1,0:T(8,128)(2,1)} %param.19) | copy-start | bytes 589828
  119.0 2.1 collective-permute-start.10
  125.4 1.3 copy-start.7
  125.4 196.2 %all-reduce.15.cloned.1.call-start = ((), (), s32[]{:S(2)}) async-start(), calls=%async_computation.4 | async-start | bytes 1769472 | tf_op jit(solution)/shard_map/psum | solution.py:66
  138.8 8.1 %collective-permute-start.3 = (f32[33,256]{1,0:T(8,128)S(1)}, f32[33,256]{1,0:T(8,128)S(1)}, u32[]{:S(2)}, u32[]{:S(2)}) collective-permute-start(f32[33,256]{1,0:T(8,128)S(1)} %bitcast.148), channel_id=1, source_target_pairs={{1,0},{2,1},{3,2},{5,4},{6,5},{7,6},{9,8},{10,9},{11,10},{13,12},{... | collective-permute-start | bytes 101384 | tf_op jit(solution)/shard_map/ppermute | solution.py:12
  142.9 127.8 %collective-permute-start.4 = (f32[96,256]{1,0:T(8,128)}, f32[96,256]{1,0:T(8,128)S(1)}, u32[]{:S(2)}, u32[]{:S(2)}) collective-permute-start(f32[96,256]{1,0:T(8,128)} %slice_bitcast_fusion.12), channel_id=1, source_target_pairs={{4,0},{5,1},{6,2},{7,3},{12,8},{13,9},{14,10},{15,11},{20,16},{21,... | collective-permute-start | bytes 294920 | tf_op jit(solution)/shard_map/ppermute | solution.py:12
  146.9 0.6 copy-start.10
  147.6 123.1 %collective-permute-start.5 = (f32[1,256]{1,0:T(1,128)S(1)}, f32[1,256]{1,0:T(1,128)S(1)}, u32[]{:S(2)}, u32[]{:S(2)}) collective-permute-start(f32[1,256]{1,0:T(1,128)S(1)} %slice.359), channel_id=1, source_target_pairs={{4,0},{5,1},{6,2},{7,3},{12,8},{13,9},{14,10},{15,11},{20,16},{21,... | collective-permute-start | bytes 3080 | tf_op jit(solution)/shard_map/ppermute | solution.py:12
  270.7 54.5 %copy-start.1 = (bf16[3,3,256,512]{3,2,1,0:T(8,128)(2,1)S(1)}, bf16[3,3,256,512]{3,2,1,0:T(8,128)(2,1)}, u32[]{:S(2)}) copy-start(bf16[3,3,256,512]{3,2,1,0:T(8,128)(2,1)} %param.21) | copy-start | bytes 7077892
Sparse Core Ops, SparseCore 0:
  110.8 56.8 reduce-scatter.2
  170.0 97.9 reduce-scatter.4
  271.2 50.3 all-reduce.14
where the time goes:
time: 335 us; the launch traced here: 332 us
  waiting for transfers between devices  168 us (50%)
  local copies, waits for them, and re-layouts  94.8 us (28%)
  starting transfers between devices  27.9 us (8%)
  other arithmetic  16.2 us (5%)
  between operations  14.4 us (4%)
  matrix products  10.6 us (3%)
    reduce_scatter x2, waiting for transfers between devices, kernel_gradient(): lax.psum_scatter(slide_sums, ('row', 'col'), scatter_dimension=0, tiled=T...  119 us
    slice x18, local copies, waits for them, and re-layouts, gather_taps(): extended[tap_row:tap_row + 2 * out_rows:2, tap_col:tap_col + 2 * out_cols:2]  53.5 us
    psum x1, waiting for transfers between devices, kernel_gradient(): lax.psum(lax.dot_general(patches, gradient, (((0,), (0,)), ((), ())), pre...  45.9 us
    ppermute x12, starting transfers between devices, shifted(): return lax.ppermute(value, axis, pairs)  27.6 us
    unnamed x44, local copies, waits for them, and re-layouts  16.4 us
    dot_general x2, matrix products, kernel_gradient(): lax.dot_general(patches, gradient, (((0,), (0,)), ((), ())), preferred_el...  7.61 us
  transfers between devices with their start and end apart: 15, of which 4 were waited for; matrix products, arithmetic and copies ran while one was open for 28% of the time, Pallas kernels for 0%

commit v1 on v0

v1 whole, which is shorter than its diff:
```python
import functools
import math

import jax
import jax.numpy as jnp
from jax import lax
from jax.experimental import pallas as pl
from jax.experimental.pallas import tpu as pltpu
from jax.sharding import PartitionSpec as P

MESH = pl.DeviceIdType.MESH
F32 = jnp.float32
BF16 = jnp.bfloat16
NAMES = ("dp", "row", "col")


def peer(**changes):
    return tuple(changes.get(name, lax.axis_index(name)) for name in NAMES)


def halo_kernel(
    rows_n, cols_n, up_ref, hid_ref, u_row, u_col, u_cor, h_row, h_col, h_cor,
    su_row, su_col, su_cor, sh_row, sh_col, sh_cor, send_sem, recv_sem,
):
    row, col = lax.axis_index("row"), lax.axis_index("col")
    has_above, has_left = row > 0, col > 0
    has_below, has_right = row < rows_n - 1, col < cols_n - 1
    barrier = pltpu.get_barrier_semaphore()
    senders = (
        (has_below, dict(row=row + 1)),
        (has_right, dict(col=col + 1)),
        (has_below & has_right, dict(row=row + 1, col=col + 1)),
    )
    targets = (
        (has_above, dict(row=row - 1)),
        (has_left, dict(col=col - 1)),
        (has_above & has_left, dict(row=row - 1, col=col - 1)),
    )
    for holds, change in senders:
        @pl.when(holds)
        def _():
            pl.semaphore_signal(barrier, inc=1, device_id=peer(**change), device_id_type=MESH)

    su_row[...] = up_ref[0, 0].astype(F32)
    sh_row[...] = hid_ref[0, 0].astype(F32)
    for i in range(su_col.shape[0]):
        su_col[i : i + 1] = up_ref[0, i].astype(F32)[0:1]
    for i in range(sh_col.shape[0]):
        sh_col[i : i + 1] = hid_ref[0, i].astype(F32)[0:1]
    su_cor[...] = up_ref[0, 0].astype(F32)[0:8]
    sh_cor[...] = hid_ref[0, 0].astype(F32)[0:8]

    above, left = has_above.astype(jnp.int32), has_left.astype(jnp.int32)

    @pl.when(has_above | has_left)
    def _():
        pl.semaphore_wait(barrier, above + left + above * left)

    pairs = (
        ((su_row, u_row), (sh_row, h_row)),
        ((su_col, u_col), (sh_col, h_col)),
        ((su_cor, u_cor), (sh_cor, h_cor)),
    )

    def copies(way, change):
        return [
            pltpu.make_async_remote_copy(
                src_ref=src, dst_ref=dst, send_sem=send_sem.at[2 * way + k],
                recv_sem=recv_sem.at[2 * way + k], device_id=peer(**change), device_id_type=MESH,
            )
            for k, (src, dst) in enumerate(pairs[way])
        ]

    for way, (holds, change) in enumerate(targets):
        @pl.when(holds)
        def _():
            for copy in copies(way, change):
                copy.start()

    for way, (holds, change) in enumerate(senders):
        @pl.when(holds)
        def _():
            for copy in copies(way, change):
                copy.wait_recv()

        @pl.when(jnp.logical_not(holds))
        def _():
            for _, dst in pairs[way]:
                dst[...] = jnp.zeros(dst.shape, dst.dtype)

    for way, (holds, change) in enumerate(targets):
        @pl.when(holds)
        def _():
            for copy in copies(way, change):
                copy.wait_send()


def exchange_halo(upstream, hidden, mesh):
    _, ur, uc, uw = upstream.shape
    _, hr, hc, hw = hidden.shape
    shapes = [(uc, uw), (ur, uw), (8, uw), (hc, hw), (hr, hw), (8, hw)]
    return pl.pallas_call(
        functools.partial(halo_kernel, mesh.shape["row"], mesh.shape["col"]),
        out_shape=[jax.ShapeDtypeStruct(s, F32) for s in shapes],
        in_specs=[pl.BlockSpec(memory_space=pltpu.VMEM)] * 2,
        out_specs=[pl.BlockSpec(memory_space=pltpu.VMEM)] * 6,
        scratch_shapes=[pltpu.VMEM(s, F32) for s in shapes]
        + [pltpu.SemaphoreType.DMA((6,)), pltpu.SemaphoreType.DMA((6,))],
        compiler_params=pltpu.CompilerParams(
            collective_id=0, has_side_effects=True, vmem_limit_bytes=16 * 2**20
        ),
    )(upstream, hidden)


TAPS = {0: ((1, 0),), 1: ((2, 0), (0, 1))}
LANE = {(0, 1): 0, (0, 0): 1, (1, 0): 2, (1, 1): 3}


def terms_of(pr, pc):
    found = []
    for a, sr in TAPS[pr]:
        for b, sc in TAPS[pc]:
            found.append((LANE[(sr, sc)], a, b, (sr, sc)))
    return sorted(found)


PARITIES = ((0, 0), (0, 1), (1, 0), (1, 1))


def dot_t(x, w):
    return lax.dot_general(x, w, (((1,), (1,)), ((), ())), preferred_element_type=F32)


def dot_0(x, y):
    return lax.dot_general(x, y, (((0,), (0,)), ((), ())), preferred_element_type=F32)


def compute_kernel(
    scale_one, scale_two, pix_ref, hid_ref, up_ref, u_row, u_col, u_cor, h_row, h_col, h_cor,
    k1_ref, k2_ref, out_ref, g_ref, uext, gext, eext, ucat, ecat, aact, pix32,
):
    _, ur, uc, uw = up_ref.shape
    _, hr, hc, hw = hid_ref.shape
    pw = pix_ref.shape[-1]
    ucp = uext.shape[1] - 8
    uext[0:ur, 0:uc] = up_ref[0].astype(F32)
    uext[ur, 0:uc] = u_row[...]
    for i in range(ur):
        uext[i, uc : uc + 1] = u_col[i : i + 1]
    uext[ur, uc : uc + 1] = u_cor[0:1]

    for (sr, sc), lane in LANE.items():
        part = uext[sr : sr + ur, sc : sc + uc].reshape(ur * uc, uw).astype(BF16)
        ucat[:, lane * uw : (lane + 1) * uw] = part

    for pr, pc in PARITIES:
        kr = ur + 1 - pr
        total = None
        for _, a, b, (sr, sc) in terms_of(pr, pc):
            u = uext[sr : sr + kr, sc : sc + ucp].reshape(kr * ucp, uw).astype(BF16)
            term = dot_t(u, k2_ref[a, b])
            total = term if total is None else total + term
        total = total.reshape(kr, ucp, hw)
        for k in range(kr):
            for lo in range(0, hw, 128):
                gext[lo // 128, 2 * k + pr, pl.ds(pc, ucp, stride=2), :] = total[k, :, lo : lo + 128]

    for p in range(hr + 1):
        hid = hid_ref[0, p].astype(F32) if p < hr else h_row[...]
        edge = h_col[p : p + 1] if p < hr else h_cor[0:1]
        for lo in range(0, hw, 128):
            cut = slice(lo, lo + 128)
            eext[p, 0:hc, cut] = jnp.where(hid[:, cut] > 0, gext[lo // 128, p, 0:hc], 0.0)
            eext[p, hc : hc + 1, cut] = jnp.where(
                edge[:, cut] > 0, gext[lo // 128, p, hc : hc + 1], 0.0
            )
            if p < hr:
                aact[lo // 128, p] = jnp.maximum(hid[:, cut], 0.0)

    for (sr, sc), lane in LANE.items():
        part = eext[sr : sr + hr, sc : sc + hc].reshape(hr * hc, hw).astype(BF16)
        ecat[:, lane * hw : (lane + 1) * hw] = part

    def put(tap, lanes, value):
        g_ref[pl.ds(tap * hw, hw), lanes] = value.astype(BF16)

    for pr, pc in PARITIES:
        parts = [
            jnp.stack([aact[h, 2 * k + pr, pl.ds(pc, uc, stride=2), :] for k in range(ur)])
            for h in range(hw // 128)
        ]
        act = jnp.concatenate(parts, axis=-1).reshape(ur * uc, hw).astype(BF16)
        terms = terms_of(pr, pc)
        first = terms[0][0]
        total = dot_0(act, ucat[:, first * uw : (first + len(terms)) * uw]) * scale_two
        for n, (_, a, b, _) in enumerate(terms):
            put(3 * a + b, pl.ds(hw, uw), total[:, n * uw : (n + 1) * uw])

    for h in range(pw // 128):
        pix32[h] = pix_ref[0, :, :, h * 128 : (h + 1) * 128].astype(F32)
    for pr, pc in PARITIES:
        parts = [
            jnp.stack([pix32[h, 2 * k + pr, pl.ds(pc, hc, stride=2), :] for k in range(hr)])
            for h in range(pw // 128)
        ]
        pix = jnp.concatenate(parts, axis=-1).reshape(hr * hc, pw).astype(BF16)
        terms = terms_of(pr, pc)
        first = terms[0][0]
        total = dot_0(pix, ecat[:, first * hw : (first + len(terms)) * hw]) * scale_one
        for n, (_, a, b, _) in enumerate(terms):
            put(3 * a + b, pl.ds(0, hw), total[:, n * hw : (n + 1) * hw])

    for pr, pc in PARITIES:
        total = None
        for lane, a, b, _ in terms_of(pr, pc):
            term = dot_t(ecat[:, lane * hw : (lane + 1) * hw], k1_ref[a, b])
            total = term if total is None else total + term
        total = total.reshape(hr, hc, pw)
        for k in range(hr):
            for h in range(pw // 128):
                pix32[h, 2 * k + pr, pl.ds(pc, hc, stride=2), :] = total[k, :, h * 128 : (h + 1) * 128]
    for h in range(pw // 128):
        out_ref[0, :, :, h * 128 : (h + 1) * 128] = pix32[h].astype(BF16)


def compute(pixels, hidden, upstream, halo, kernel_first, kernel_second, devices):
    _, ur, uc, uw = upstream.shape
    _, hr, hc, hw = hidden.shape
    _, pr, pc, pw = pixels.shape
    scale_one = 1.0 / math.sqrt(devices * hr * hc)
    scale_two = 1.0 / math.sqrt(devices * ur * uc)
    ucp = (uc // 8 + 1) * 8
    vmem = pl.BlockSpec(memory_space=pltpu.VMEM)
    return pl.pallas_call(
        functools.partial(compute_kernel, scale_one, scale_two),
        out_shape=[
            jax.ShapeDtypeStruct(pixels.shape, BF16),
            jax.ShapeDtypeStruct((9 * hw, hw + uw), BF16),
        ],
        in_specs=[vmem] * 11,
        out_specs=[vmem] * 2,
        scratch_shapes=[
            pltpu.VMEM((ur + 2, ucp + 8, uw), F32),
            pltpu.VMEM((hw // 128, hr + 2, 2 * ucp, 128), F32),
            pltpu.VMEM((hr + 1, hc + 8, hw), F32),
            pltpu.VMEM((ur * uc, 4 * uw), BF16),
            pltpu.VMEM((hr * hc, 4 * hw), BF16),
            pltpu.VMEM((hw // 128, hr, hc, 128), F32),
            pltpu.VMEM((pw // 128, pr, pc, 128), F32),
        ],
        compiler_params=pltpu.CompilerParams(vmem_limit_bytes=52 * 2**20),
    )(pixels, hidden, upstream, *halo, kernel_first, kernel_second)


def reduce_kernel(
    dps, rows_n, cols_n, g_ref, out_ref, acc1, in1, acc2, in2, in3, mine, in4,
    s1, r1, s2, r2, s3, r3, s4, r4,
):
    dp, row, col = (lax.axis_index(name) for name in NAMES)
    size, width = g_ref.shape[2:]
    half, lanes = size // 2, width // 2
    barrier = pltpu.get_barrier_semaphore()
    partners = (
        [dict(row=lax.rem(row + k, rows_n)) for k in range(1, rows_n)]
        + [dict(dp=lax.rem(dp + k, dps)) for k in range(1, dps)]
        + [dict(col=lax.rem(col + k, cols_n)) for k in range(1, cols_n)]
    )
    for change in partners:
        pl.semaphore_signal(barrier, inc=1, device_id=peer(**change), device_id_type=MESH)
    pl.semaphore_wait(barrier, len(partners))

    def remote(src, dst, send, recv, change):
        return pltpu.make_async_remote_copy(
            src_ref=src, dst_ref=dst, send_sem=send, recv_sem=recv,
            device_id=peer(**change), device_id_type=MESH,
        )

    def piece(ref, d):
        return ref.at[d // 2, d % 2]

    def target(me, k, n):
        return lax.rem(me + k, n)

    copies1, copies2, copies3, copies4 = {}, {}, {}, {}
    order = [lax.rem(col + j, cols_n) for j in range(1, cols_n)] + [col]
    for j, c in enumerate(order):
        for k in range(1, rows_n):
            to = target(row, k, rows_n)
            copy = remote(
                g_ref.at[to, c], in1.at[k - 1, j], s1.at[k - 1, j], r1.at[k - 1, j], dict(row=to)
            )
            copy.start()
            copies1[k, j] = copy
    for j, c in enumerate(order):
        for k in range(1, rows_n):
            copies1[k, j].wait_recv()
        total = g_ref[row, c].astype(F32)
        for k in range(1, rows_n):
            total = total + in1[k - 1, j].astype(F32)
        for y in range(2):
            for x in range(2):
                acc1[j, y, x] = total[y * half : (y + 1) * half, x * lanes : (x + 1) * lanes].astype(BF16)
        for k in range(1, dps):
            to = target(dp, k, dps)
            copy = remote(
                acc1.at[j, to // 2, to % 2], in2.at[k - 1, j], s2.at[k - 1, j], r2.at[k - 1, j],
                dict(dp=to),
            )
            copy.start()
            copies2[k, j] = copy
    for j, c in enumerate(order):
        for k in range(1, dps):
            copies2[k, j].wait_recv()
        total = acc1[j, dp // 2, dp % 2].astype(F32)
        for k in range(1, dps):
            total = total + in2[k - 1, j].astype(F32)
        acc2[j] = total.astype(BF16)
        if j < cols_n - 1:
            copy = remote(acc2.at[j], in3.at[j], s3.at[j], r3.at[j], dict(col=c))
            copy.start()
            copies3[j] = copy
    total = acc2[cols_n - 1].astype(F32)
    for j in range(cols_n - 1):
        copies3[j].wait_recv()
        total = total + in3[j].astype(F32)
    mine[...] = total.astype(BF16)
    for k in range(1, dps):
        to = target(dp, k, dps)
        copy = remote(mine, in4.at[dp // 2, dp % 2], s4.at[k - 1], r4.at[k - 1], dict(dp=to))
        copy.start()
        copies4[k] = copy
    in4[dp // 2, dp % 2] = mine[...]
    for k in range(1, dps):
        copies4[k].wait_recv()
    for y in range(2):
        for x in range(2):
            out_ref[y * half : (y + 1) * half, x * lanes : (x + 1) * lanes] = in4[y, x].astype(F32)
    for group in (copies1, copies2, copies3, copies4):
        for copy in group.values():
            copy.wait_send()


def reduce_gradients(g, mesh, shares):
    dps, rows_n, cols_n = (mesh.shape[name] for name in NAMES)
    size = g.shape[0] // shares
    padded = -(-size // 32) * 32
    width = g.shape[1]
    g = g.reshape(shares, size, width)
    if padded != size:
        g = jnp.pad(g, ((0, 0), (0, padded - size), (0, 0)))
    g = g.reshape(rows_n, cols_n, padded, width)
    half, lanes = padded // 2, width // 2
    dma = pltpu.SemaphoreType.DMA
    out = pl.pallas_call(
        functools.partial(reduce_kernel, dps, rows_n, cols_n),
        out_shape=jax.ShapeDtypeStruct((padded, width), F32),
        in_specs=[pl.BlockSpec(memory_space=pltpu.VMEM)],
        out_specs=pl.BlockSpec(memory_space=pltpu.VMEM),
        scratch_shapes=[
            pltpu.VMEM((cols_n, 2, 2, half, lanes), BF16),
            pltpu.VMEM((rows_n - 1, cols_n, padded, width), BF16),
            pltpu.VMEM((cols_n, half, lanes), BF16),
            pltpu.VMEM((dps - 1, cols_n, half, lanes), BF16),
            pltpu.VMEM((cols_n - 1, half, lanes), BF16),
            pltpu.VMEM((half, lanes), BF16),
            pltpu.VMEM((2, 2, half, lanes), BF16),
            dma((rows_n - 1, cols_n)), dma((rows_n - 1, cols_n)),
            dma((dps - 1, cols_n)), dma((dps - 1, cols_n)),
            dma((cols_n - 1,)), dma((cols_n - 1,)),
            dma((dps - 1,)), dma((dps - 1,)),
        ],
        compiler_params=pltpu.CompilerParams(
            collective_id=1, has_side_effects=True, vmem_limit_bytes=48 * 2**20
        ),
    )(g)
    return out[:size]


def solution(mesh):
    def per_device(pixels, hidden, upstream, kernel_first, kernel_second):
        devices = mesh.size
        shares = mesh.shape["row"] * mesh.shape["col"]
        halo = exchange_halo(upstream, hidden, mesh)
        grad_pixels, gradients = compute(
            pixels, hidden, upstream, halo, kernel_first, kernel_second, devices
        )
        total = reduce_gradients(gradients, mesh, shares)
        width = kernel_first.shape[-1]
        return grad_pixels, total[:, :width], total[:, width:]

    in_specs = (P("dp", "row", "col", None),) * 3 + (P(), P())
    out_specs = (P("dp", "row", "col", None), P(("row", "col"), None), P(("row", "col"), None))
    return jax.shard_map(
        per_device, mesh=mesh, in_specs=in_specs, out_specs=out_specs, check_vma=False
    )
```

time: 335 us -> 56.1 us (0.17)
  waiting for transfers between devices: 168 us -> 0 us
  local copies, waits for them, and re-layouts: 94.8 us -> 8.73 us
  Pallas kernels: 0 us -> 46.3 us
  starting transfers between devices: 27.9 us -> 0 us
  other arithmetic: 16.2 us -> 0 us
  between operations: 14.4 us -> 0.67 us
  matrix products: 10.6 us -> 0 us
    reduce_scatter x2 -> x0, waiting for transfers between devices: 119 us -> none  [kernel_gradient(): lax.psum_scatter(slide_sums, ('row', 'col'), scatter_dimension=0, tiled=T...]
    slice x28 -> x2, local copies, waits for them, and re-layouts: 58.3 us -> 1.63 us  [per_device(): return (grad_pixels, total[:, :width], total[:, width:])]
    pallas_call x0 -> x3, Pallas kernels: none -> 46.3 us  [the longest x1 33.1 us: reduce_gradients(): pl.pallas_call(functools.partial(reduce_kernel, dps, rows_n, cols_n), out...]
    psum x1 -> x0, waiting for transfers between devices: 45.9 us -> none  [kernel_gradient(): lax.psum(lax.dot_general(patches, gradient, (((0,), (0,)), ((), ())), pre...]
    ppermute x12 -> x0, starting transfers between devices: 27.6 us -> none  [shifted(): return lax.ppermute(value, axis, pairs)]
    dot_general x4 -> x0, matrix products: 10.6 us -> none  [the longest x2 7.61 us: kernel_gradient(): lax.dot_general(patches, gradient, (((0,), (0,)), ((), ())), preferred_el...]
    unnamed x44 -> x12, local copies, waits for them, and re-layouts: 16.4 us -> 7.11 us
    another operation x9 -> x0, local copies, waits for them, and re-layouts: 6.13 us -> none  [the longest x4 5.18 us: spread_taps(): jnp.stack([even_part, odd_part], axis=2)]
  transfers between devices with their start and end apart: 15 -> 0, of which waited for: 4 -> 0; matrix products, arithmetic and copies ran while one was open for 28% -> 0% of each run, Pallas kernels for 0% -> 0%
where the time goes in v1:
time: 56.1 us; the launch traced here: 55.7 us
  Pallas kernels  46.3 us (83%)
  local copies, waits for them, and re-layouts  8.73 us (16%)
  between operations  0.67 us (1%)
    pallas_call x1, Pallas kernels, reduce_gradients(): pl.pallas_call(functools.partial(reduce_kernel, dps, rows_n, cols_n), out...  33.1 us
    pallas_call x1, Pallas kernels, compute(): pl.pallas_call(functools.partial(compute_kernel, scale_one, scale_two), o...  7.81 us
    unnamed x12, local copies, waits for them, and re-layouts  7.11 us
    pallas_call x1, Pallas kernels, exchange_halo(): pl.pallas_call(functools.partial(halo_kernel, mesh.shape['row'], mesh.sha...  5.45 us
    slice x2, local copies, waits for them, and re-layouts, per_device(): return (grad_pixels, total[:, :width], total[:, width:])  1.63 us

profile of v1, /device:TPU:0, one launch (start us, length us, event | category | flops | bytes accessed | tf_op | source)
XLA Modules:
  0.0 55.7 jit_solution(13377898659404039259)
XLA Ops:
  0.6 0.0 copy-start.1
  0.6 1.0 %copy-done.1 = bf16[1,16,48,256]{3,2,1,0:T(8,128)(2,1)S(1)} copy-done((bf16[1,16,48,256]{3,2,1,0:T(8,128)(2,1)S(1)}, bf16[1,16,48,256]{3,2,1,0:T(8,128)(2,1)}, u32[]{:S(2)}) %copy-start.1) | copy-done | bytes 393240
  1.6 0.0 copy-start.4
  1.6 0.9 %copy-done.4 = bf16[1,8,24,512]{3,2,1,0:T(8,128)(2,1)S(1)} copy-done((bf16[1,8,24,512]{3,2,1,0:T(8,128)(2,1)S(1)}, bf16[1,8,24,512]{3,2,1,0:T(8,128)(2,1)}, u32[]{:S(2)}) %copy-start.4) | copy-done | bytes 196632
  2.6 5.5 %shard_map.76 = (f32[24,512]{1,0:T(8,128)S(1)}, f32[8,512]{1,0:T(8,128)S(1)}, f32[8,512]{1,0:T(8,128)S(1)}, f32[48,256]{1,0:T(8,128)S(1)}, f32[16,256]{1,0:T(8,128)S(1)}, /*index=5*/f32[8,256]{1,0:T(8,128)S(1)}) custom-call(bf16[1,8,24,512]{3,2,1,0:T(8,128)(2,1)S(1)} %copy-done.4, bf16[1,16,48,256]{3,2,1,0:T(8,128)(2,1)S(1)} %copy-done.1), custom_call_target="tpu_custom_call" | custom-call | tf_op jit(solution)/shard_map/pallas_call | solution.py:102
  8.0 0.0 copy-start.2
  8.0 1.0 %copy-done.2 = bf16[1,16,48,256]{3,2,1,0:T(8,128)(2,1)S(1)} copy-done((bf16[1,16,48,256]{3,2,1,0:T(8,128)(2,1)S(1)}, bf16[1,16,48,256]{3,2,1,0:T(8,128)(2,1)}, u32[]{:S(2)}) %copy-start.2) | copy-done | bytes 393240
  9.0 0.0 copy-start.3
  9.0 1.3 %copy-done.3 = bf16[3,3,256,256]{3,2,1,0:T(8,128)(2,1)S(1)} copy-done((bf16[3,3,256,256]{3,2,1,0:T(8,128)(2,1)S(1)}, bf16[3,3,256,256]{3,2,1,0:T(8,128)(2,1)}, u32[]{:S(2)}) %copy-start.3) | copy-done | bytes 1179672
  10.3 0.0 copy-start.5
  10.3 0.9 %copy-done.5 = bf16[1,8,24,512]{3,2,1,0:T(8,128)(2,1)S(1)} copy-done((bf16[1,8,24,512]{3,2,1,0:T(8,128)(2,1)S(1)}, bf16[1,8,24,512]{3,2,1,0:T(8,128)(2,1)}, u32[]{:S(2)}) %copy-start.5) | copy-done | bytes 196632
  11.2 7.8 %shard_map.77 = (bf16[1,32,96,256]{3,2,1,0:T(8,128)(2,1)}, bf16[2304,768]{1,0:T(8,128)(2,1)}) custom-call(bf16[1,32,96,256]{3,2,1,0:T(8,128)(2,1)} %pix_ref.1, bf16[1,16,48,256]{3,2,1,0:T(8,128)(2,1)S(1)} %copy-done.2, bf16[1,8,24,512]{3,2,1,0:T(8,128)(2,1)S(1)} %copy-done.5, f32[24,512]{1,0:T(8,128)S(1)} %get-tuple-element.11.u_row, ...), custom_call_target="tpu_custom_call" | custom-call | tf_op jit(solution)/shard_map/pallas_call | solution.py:234
  19.0 0.0 copy-start
  19.0 2.0 %copy-done = bf16[2304,768]{1,0:T(8,128)(2,1)S(1)} copy-done((bf16[2304,768]{1,0:T(8,128)(2,1)S(1)}, bf16[2304,768]{1,0:T(8,128)(2,1)}, u32[]{:S(2)}) %copy-start) | copy-done | bytes 3538968
  21.0 33.1 %shard_map.78 = f32[288,768]{1,0:T(8,128)S(1)} custom-call(bf16[2,4,288,768]{3,2,1,0:T(8,128)(2,1)S(1)} %bitcast.1), custom_call_target="tpu_custom_call" | custom-call | tf_op jit(solution)/shard_map/pallas_call | solution.py:354
  54.1 0.7 %slice.6 = f32[288,256]{1,0:T(8,128)} slice(f32[288,768]{1,0:T(8,128)S(1)} %shard_map.78), slice={[0:288], [0:256]} | slice | bytes 589824 | tf_op jit(solution)/shard_map/slice | solution.py:389
  54.8 0.9 %slice.7 = f32[288,512]{1,0:T(8,128)} slice(f32[288,768]{1,0:T(8,128)S(1)} %shard_map.78), slice={[0:288], [256:768]} | slice | bytes 1179648 | tf_op jit(solution)/shard_map/slice | solution.py:389
Async XLA Ops:
  0.6 1.0 %copy-start.1 = (bf16[1,16,48,256]{3,2,1,0:T(8,128)(2,1)S(1)}, bf16[1,16,48,256]{3,2,1,0:T(8,128)(2,1)}, u32[]{:S(2)}) copy-start(bf16[1,16,48,256]{3,2,1,0:T(8,128)(2,1)} %hid_ref.3) | copy-start | bytes 1179652
  1.6 0.9 %copy-start.4 = (bf16[1,8,24,512]{3,2,1,0:T(8,128)(2,1)S(1)}, bf16[1,8,24,512]{3,2,1,0:T(8,128)(2,1)}, u32[]{:S(2)}) copy-start(bf16[1,8,24,512]{3,2,1,0:T(8,128)(2,1)} %up_ref.3) | copy-start | bytes 589828
  8.0 1.0 %copy-start.2 = (bf16[1,16,48,256]{3,2,1,0:T(8,128)(2,1)S(1)}, bf16[1,16,48,256]{3,2,1,0:T(8,128)(2,1)}, u32[]{:S(2)}) copy-start(bf16[1,16,48,256]{3,2,1,0:T(8,128)(2,1)} %hid_ref.3) | copy-start | bytes 1179652
  9.0 1.3 %copy-start.3 = (bf16[3,3,256,256]{3,2,1,0:T(8,128)(2,1)S(1)}, bf16[3,3,256,256]{3,2,1,0:T(8,128)(2,1)}, u32[]{:S(2)}) copy-start(bf16[3,3,256,256]{3,2,1,0:T(8,128)(2,1)} %k1_ref.1) | copy-start | bytes 3538948
  10.3 0.9 %copy-start.5 = (bf16[1,8,24,512]{3,2,1,0:T(8,128)(2,1)S(1)}, bf16[1,8,24,512]{3,2,1,0:T(8,128)(2,1)}, u32[]{:S(2)}) copy-start(bf16[1,8,24,512]{3,2,1,0:T(8,128)(2,1)} %up_ref.3) | copy-start | bytes 589828
  19.0 2.0 %copy-start = (bf16[2304,768]{1,0:T(8,128)(2,1)S(1)}, bf16[2304,768]{1,0:T(8,128)(2,1)}, u32[]{:S(2)}) copy-start(bf16[2304,768]{1,0:T(8,128)(2,1)} %get-tuple-element.18) | copy-start | bytes 10616836

commit v2 on v1

--- a/solution.py
+++ b/solution.py
@@ -253,12 +253,14 @@
 
 
 def reduce_kernel(
-    dps, rows_n, cols_n, g_ref, out_ref, acc1, in1, acc2, in2, in3, mine, in4,
-    s1, r1, s2, r2, s3, r3, s4, r4,
+    dps, rows_n, cols_n, g_ref, out_ref, acc1, in1, acc_a, in_a, acc_b, in_b, in3, mine, in4,
+    s1, r1, sa, ra, sb, rb, s3, r3, s4, r4,
 ):
     dp, row, col = (lax.axis_index(name) for name in NAMES)
     size, width = g_ref.shape[2:]
     half, lanes = size // 2, width // 2
+    bits = (dp // 2, dp % 2)
+    across = (dict(dp=lax.rem(dp + 2, 4)), dict(dp=dp + 1 - 2 * (dp % 2)))
     barrier = pltpu.get_barrier_semaphore()
     partners = (
         [dict(row=lax.rem(row + k, rows_n)) for k in range(1, rows_n)]
@@ -268,76 +270,87 @@
     for change in partners:
         pl.semaphore_signal(barrier, inc=1, device_id=peer(**change), device_id_type=MESH)
     pl.semaphore_wait(barrier, len(partners))
-
-    def remote(src, dst, send, recv, change):
-        return pltpu.make_async_remote_copy(
-            src_ref=src, dst_ref=dst, send_sem=send, recv_sem=recv,
+    started = []
+
+    def send(src, dst, send_sem, recv_sem, change):
+        copy = pltpu.make_async_remote_copy(
+            src_ref=src, dst_ref=dst, send_sem=send_sem, recv_sem=recv_sem,
             device_id=peer(**change), device_id_type=MESH,
         )
-
-    def piece(ref, d):
-        return ref.at[d // 2, d % 2]
-
-    def target(me, k, n):
-        return lax.rem(me + k, n)
-
-    copies1, copies2, copies3, copies4 = {}, {}, {}, {}
+        copy.start()
+        started.append(copy)
+        return copy
+
+    copies1, copies_a, copies_b, copies3, copies4 = {}, {}, {}, {}, {}
     order = [lax.rem(col + j, cols_n) for j in range(1, cols_n)] + [col]
     for j, c in enumerate(order):
         for k in range(1, rows_n):
-            to = target(row, k, rows_n)
-            copy = remote(
+            to = lax.rem(row + k, rows_n)
+            copies1[k, j] = send(
                 g_ref.at[to, c], in1.at[k - 1, j], s1.at[k - 1, j], r1.at[k - 1, j], dict(row=to)
             )
-            copy.start()
-            copies1[k, j] = copy
-    for j, c in enumerate(order):
+
+    def first_stage(j):
         for k in range(1, rows_n):
             copies1[k, j].wait_recv()
-        total = g_ref[row, c].astype(F32)
-        for k in range(1, rows_n):
-            total = total + in1[k - 1, j].astype(F32)
         for y in range(2):
             for x in range(2):
-                acc1[j, y, x] = total[y * half : (y + 1) * half, x * lanes : (x + 1) * lanes].astype(BF16)
-        for k in range(1, dps):
-            to = target(dp, k, dps)
-            copy = remote(
-                acc1.at[j, to // 2, to % 2], in2.at[k - 1, j], s2.at[k - 1, j], r2.at[k - 1, j],
-                dict(dp=to),
-            )
-            copy.start()
-            copies2[k, j] = copy
-    for j, c in enumerate(order):
-        for k in range(1, dps):
-            copies2[k, j].wait_recv()
-        total = acc1[j, dp // 2, dp % 2].astype(F32)
-        for k in range(1, dps):
-            total = total + in2[k - 1, j].astype(F32)
-        acc2[j] = total.astype(BF16)
-        if j < cols_n - 1:
-            copy = remote(acc2.at[j], in3.at[j], s3.at[j], r3.at[j], dict(col=c))
-            copy.start()
-            copies3[j] = copy
-    total = acc2[cols_n - 1].astype(F32)
+                rows, cut = pl.ds(y * half, half), pl.ds(x * lanes, lanes)
+                total = g_ref[row, order[j], rows, cut].astype(F32)
+                for k in range(1, rows_n):
+                    total = total + in1[k - 1, j, rows, cut].astype(F32)
+                at = (y, x) if j % 2 == 0 else (x, y)
+                acc1[j, at[0], at[1]] = total.astype(BF16)
+        way = j % 2
+        copies_a[j] = send(
+            acc1.at[j, 1 - bits[way]], in_a.at[j], sa.at[j], ra.at[j], across[way]
+        )
+
+    def second_stage(j):
+        way = j % 2
+        copies_a[j].wait_recv()
+        there = 1 - bits[1 - way]
+        acc_a[j] = (
+            acc1[j, bits[way], there].astype(F32) + in_a[j, there].astype(F32)
+        ).astype(BF16)
+        copies_b[j] = send(acc_a.at[j], in_b.at[j], sb.at[j], rb.at[j], across[1 - way])
+
+    def third_stage(j):
+        way = j % 2
+        here = bits[1 - way]
+        total = acc1[j, bits[way], here].astype(F32) + in_a[j, here].astype(F32)
+        copies_b[j].wait_recv()
+        total = total + in_b[j].astype(F32)
+        if j == cols_n - 1:
+            return total
+        acc_b[j] = total.astype(BF16)
+        copies3[j] = send(acc_b.at[j], in3.at[j], s3.at[j], r3.at[j], dict(col=order[j]))
+
+    total = None
+    for step in range(cols_n + 3):
+        if step < cols_n:
+            first_stage(step)
+        if 0 <= step - 2 < cols_n:
+            second_stage(step - 2)
+        if 0 <= step - 3 < cols_n:
+            total = third_stage(step - 3)
     for j in range(cols_n - 1):
         copies3[j].wait_recv()
         total = total + in3[j].astype(F32)
     mine[...] = total.astype(BF16)
     for k in range(1, dps):
-        to = target(dp, k, dps)
-        copy = remote(mine, in4.at[dp // 2, dp % 2], s4.at[k - 1], r4.at[k - 1], dict(dp=to))
-        copy.start()
-        copies4[k] = copy
-    in4[dp // 2, dp % 2] = mine[...]
+        to = lax.rem(dp + k, dps)
+        copies4[k] = send(
+            mine, in4.at[bits[0], bits[1]], s4.at[k - 1], r4.at[k - 1], dict(dp=to)
+        )
+    in4[bits[0], bits[1]] = mine[...]
     for k in range(1, dps):
         copies4[k].wait_recv()
     for y in range(2):
         for x in range(2):
             out_ref[y * half : (y + 1) * half, x * lanes : (x + 1) * lanes] = in4[y, x].astype(F32)
-    for group in (copies1, copies2, copies3, copies4):
-        for copy in group.values():
-            copy.wait_send()
+    for copy in started:
+        copy.wait_send()
 
 
 def reduce_gradients(g, mesh, shares):
@@ -360,12 +373,14 @@
             pltpu.VMEM((cols_n, 2, 2, half, lanes), BF16),
             pltpu.VMEM((rows_n - 1, cols_n, padded, width), BF16),
             pltpu.VMEM((cols_n, half, lanes), BF16),
-            pltpu.VMEM((dps - 1, cols_n, half, lanes), BF16),
+            pltpu.VMEM((cols_n, 2, half, lanes), BF16),
+            pltpu.VMEM((cols_n - 1, half, lanes), BF16),
+            pltpu.VMEM((cols_n, half, lanes), BF16),
             pltpu.VMEM((cols_n - 1, half, lanes), BF16),
             pltpu.VMEM((half, lanes), BF16),
             pltpu.VMEM((2, 2, half, lanes), BF16),
             dma((rows_n - 1, cols_n)), dma((rows_n - 1, cols_n)),
-            dma((dps - 1, cols_n)), dma((dps - 1, cols_n)),
+            dma((cols_n,)), dma((cols_n,)), dma((cols_n,)), dma((cols_n,)),
             dma((cols_n - 1,)), dma((cols_n - 1,)),
             dma((dps - 1,)), dma((dps - 1,)),
         ],

time: 56.1 us -> 57.6 us (1.027)
  Pallas kernels: 46.3 us -> 47.8 us
    pallas_call x1, Pallas kernels: 33.1 us -> 34.6 us  [reduce_gradients(): pl.pallas_call(functools.partial(reduce_kernel, dps, rows_n, cols_n), out...]
where the time goes in v2:
time: 57.6 us; the launch traced here: 57.2 us
  Pallas kernels  47.8 us (83%)
  local copies, waits for them, and re-layouts  8.73 us (15%)
  between operations  0.67 us (1%)
    pallas_call x1, Pallas kernels, reduce_gradients(): pl.pallas_call(functools.partial(reduce_kernel, dps, rows_n, cols_n), out...  34.6 us
    pallas_call x1, Pallas kernels, compute(): pl.pallas_call(functools.partial(compute_kernel, scale_one, scale_two), o...  7.81 us
    unnamed x12, local copies, waits for them, and re-layouts  7.11 us
    pallas_call x1, Pallas kernels, exchange_halo(): pl.pallas_call(functools.partial(halo_kernel, mesh.shape['row'], mesh.sha...  5.45 us
    slice x2, local copies, waits for them, and re-layouts, per_device(): return (grad_pixels, total[:, :width], total[:, width:])  1.63 us

profile of v2, /device:TPU:0, one launch (start us, length us, event | category | flops | bytes accessed | tf_op | source)
XLA Modules:
  0.0 57.2 jit_solution(14038097638725256085)
XLA Ops:
  0.6 0.0 copy-start.1
  0.6 1.0 %copy-done.1 = bf16[1,16,48,256]{3,2,1,0:T(8,128)(2,1)S(1)} copy-done((bf16[1,16,48,256]{3,2,1,0:T(8,128)(2,1)S(1)}, bf16[1,16,48,256]{3,2,1,0:T(8,128)(2,1)}, u32[]{:S(2)}) %copy-start.1) | copy-done | bytes 393240
  1.6 0.0 copy-start.4
  1.6 0.9 %copy-done.4 = bf16[1,8,24,512]{3,2,1,0:T(8,128)(2,1)S(1)} copy-done((bf16[1,8,24,512]{3,2,1,0:T(8,128)(2,1)S(1)}, bf16[1,8,24,512]{3,2,1,0:T(8,128)(2,1)}, u32[]{:S(2)}) %copy-start.4) | copy-done | bytes 196632
  2.6 5.5 %shard_map.76 = (f32[24,512]{1,0:T(8,128)S(1)}, f32[8,512]{1,0:T(8,128)S(1)}, f32[8,512]{1,0:T(8,128)S(1)}, f32[48,256]{1,0:T(8,128)S(1)}, f32[16,256]{1,0:T(8,128)S(1)}, /*index=5*/f32[8,256]{1,0:T(8,128)S(1)}) custom-call(bf16[1,8,24,512]{3,2,1,0:T(8,128)(2,1)S(1)} %copy-done.4, bf16[1,16,48,256]{3,2,1,0:T(8,128)(2,1)S(1)} %copy-done.1), custom_call_target="tpu_custom_call" | custom-call | tf_op jit(solution)/shard_map/pallas_call | solution.py:102
  8.0 0.0 copy-start.2
  8.0 1.0 %copy-done.2 = bf16[1,16,48,256]{3,2,1,0:T(8,128)(2,1)S(1)} copy-done((bf16[1,16,48,256]{3,2,1,0:T(8,128)(2,1)S(1)}, bf16[1,16,48,256]{3,2,1,0:T(8,128)(2,1)}, u32[]{:S(2)}) %copy-start.2) | copy-done | bytes 393240
  9.0 0.0 copy-start.3
  9.0 1.3 %copy-done.3 = bf16[3,3,256,256]{3,2,1,0:T(8,128)(2,1)S(1)} copy-done((bf16[3,3,256,256]{3,2,1,0:T(8,128)(2,1)S(1)}, bf16[3,3,256,256]{3,2,1,0:T(8,128)(2,1)}, u32[]{:S(2)}) %copy-start.3) | copy-done | bytes 1179672
  10.3 0.0 copy-start.5
  10.3 0.9 %copy-done.5 = bf16[1,8,24,512]{3,2,1,0:T(8,128)(2,1)S(1)} copy-done((bf16[1,8,24,512]{3,2,1,0:T(8,128)(2,1)S(1)}, bf16[1,8,24,512]{3,2,1,0:T(8,128)(2,1)}, u32[]{:S(2)}) %copy-start.5) | copy-done | bytes 196632
  11.2 7.8 %shard_map.77 = (bf16[1,32,96,256]{3,2,1,0:T(8,128)(2,1)}, bf16[2304,768]{1,0:T(8,128)(2,1)}) custom-call(bf16[1,32,96,256]{3,2,1,0:T(8,128)(2,1)} %pix_ref.1, bf16[1,16,48,256]{3,2,1,0:T(8,128)(2,1)S(1)} %copy-done.2, bf16[1,8,24,512]{3,2,1,0:T(8,128)(2,1)S(1)} %copy-done.5, f32[24,512]{1,0:T(8,128)S(1)} %get-tuple-element.11.u_row, ...), custom_call_target="tpu_custom_call" | custom-call | tf_op jit(solution)/shard_map/pallas_call | solution.py:234
  19.0 0.0 copy-start
  19.0 2.0 %copy-done = bf16[2304,768]{1,0:T(8,128)(2,1)S(1)} copy-done((bf16[2304,768]{1,0:T(8,128)(2,1)S(1)}, bf16[2304,768]{1,0:T(8,128)(2,1)}, u32[]{:S(2)}) %copy-start) | copy-done | bytes 3538968
  21.0 34.6 %shard_map.78 = f32[288,768]{1,0:T(8,128)S(1)} custom-call(bf16[2,4,288,768]{3,2,1,0:T(8,128)(2,1)S(1)} %bitcast.1), custom_call_target="tpu_custom_call" | custom-call | tf_op jit(solution)/shard_map/pallas_call | solution.py:367
  55.6 0.7 %slice.6 = f32[288,256]{1,0:T(8,128)} slice(f32[288,768]{1,0:T(8,128)S(1)} %shard_map.78), slice={[0:288], [0:256]} | slice | bytes 589824 | tf_op jit(solution)/shard_map/slice | solution.py:404
  56.3 0.9 %slice.7 = f32[288,512]{1,0:T(8,128)} slice(f32[288,768]{1,0:T(8,128)S(1)} %shard_map.78), slice={[0:288], [256:768]} | slice | bytes 1179648 | tf_op jit(solution)/shard_map/slice | solution.py:404
Async XLA Ops:
  0.6 1.0 %copy-start.1 = (bf16[1,16,48,256]{3,2,1,0:T(8,128)(2,1)S(1)}, bf16[1,16,48,256]{3,2,1,0:T(8,128)(2,1)}, u32[]{:S(2)}) copy-start(bf16[1,16,48,256]{3,2,1,0:T(8,128)(2,1)} %hid_ref.3) | copy-start | bytes 1179652
  1.6 0.9 %copy-start.4 = (bf16[1,8,24,512]{3,2,1,0:T(8,128)(2,1)S(1)}, bf16[1,8,24,512]{3,2,1,0:T(8,128)(2,1)}, u32[]{:S(2)}) copy-start(bf16[1,8,24,512]{3,2,1,0:T(8,128)(2,1)} %up_ref.3) | copy-start | bytes 589828
  8.0 1.0 %copy-start.2 = (bf16[1,16,48,256]{3,2,1,0:T(8,128)(2,1)S(1)}, bf16[1,16,48,256]{3,2,1,0:T(8,128)(2,1)}, u32[]{:S(2)}) copy-start(bf16[1,16,48,256]{3,2,1,0:T(8,128)(2,1)} %hid_ref.3) | copy-start | bytes 1179652
  9.0 1.3 %copy-start.3 = (bf16[3,3,256,256]{3,2,1,0:T(8,128)(2,1)S(1)}, bf16[3,3,256,256]{3,2,1,0:T(8,128)(2,1)}, u32[]{:S(2)}) copy-start(bf16[3,3,256,256]{3,2,1,0:T(8,128)(2,1)} %k1_ref.1) | copy-start | bytes 3538948
  10.3 0.9 %copy-start.5 = (bf16[1,8,24,512]{3,2,1,0:T(8,128)(2,1)S(1)}, bf16[1,8,24,512]{3,2,1,0:T(8,128)(2,1)}, u32[]{:S(2)}) copy-start(bf16[1,8,24,512]{3,2,1,0:T(8,128)(2,1)} %up_ref.3) | copy-start | bytes 589828
  19.0 2.0 %copy-start = (bf16[2304,768]{1,0:T(8,128)(2,1)S(1)}, bf16[2304,768]{1,0:T(8,128)(2,1)}, u32[]{:S(2)}) copy-start(bf16[2304,768]{1,0:T(8,128)(2,1)} %get-tuple-element.18) | copy-start | bytes 10616836

commit v3 on v0

v3 whole, which is shorter than its diff:
```python
import functools
import math

import jax
import jax.numpy as jnp
from jax import lax
from jax.experimental import pallas as pl
from jax.experimental.pallas import tpu as pltpu
from jax.sharding import PartitionSpec as P

MESH = pl.DeviceIdType.MESH
F32 = jnp.float32
BF16 = jnp.bfloat16
NAMES = ("dp", "row", "col")


def peer(**changes):
    return tuple(changes.get(name, lax.axis_index(name)) for name in NAMES)


TAPS = {0: ((1, 0),), 1: ((2, 0), (0, 1))}
LANE = {(0, 1): 0, (0, 0): 1, (1, 0): 2, (1, 1): 3}


def terms_of(pr, pc):
    found = []
    for a, sr in TAPS[pr]:
        for b, sc in TAPS[pc]:
            found.append((LANE[(sr, sc)], a, b, (sr, sc)))
    return sorted(found)


PARITIES = ((0, 0), (0, 1), (1, 0), (1, 1))


def dot_t(x, w):
    return lax.dot_general(x, w, (((1,), (1,)), ((), ())), preferred_element_type=F32)


def dot_0(x, y):
    return lax.dot_general(x, y, (((0,), (0,)), ((), ())), preferred_element_type=F32)


def fused_kernel(
    dps, rows_n, cols_n, share, padded, scale_one, scale_two,
    pix_hbm, hid_hbm, up_hbm, k1_hbm, k2_hbm, out_hbm, g1_out, g2_out,
    pix_ref, hid_ref, up_ref, k1_ref, k2_ref, out_ref,
    u_row, u_col, u_cor, h_row, h_col, h_cor,
    su_row, su_col, su_cor, sh_row, sh_col, sh_cor,
    uext, gext, eext, ucat, ecat, aact, pix32, g_ref,
    acc1, in1, acc2, in2, in3, mine, in4,
    local_sem, halo_send, halo_recv, s1, r1, s2, r2, s3, r3, s4, r4,
):
    dp, row, col = (lax.axis_index(name) for name in NAMES)
    _, ur, uc, uw = up_ref.shape
    _, hr, hc, hw = hid_ref.shape
    pw = pix_ref.shape[-1]
    ucp = uext.shape[1] - 8
    width = hw + uw
    half, lanes = padded // 2, width // 2
    local = [
        pltpu.make_async_copy(src, dst, local_sem.at[n])
        for n, (src, dst) in enumerate(
            ((up_hbm, up_ref), (hid_hbm, hid_ref), (pix_hbm, pix_ref), (k2_hbm, k2_ref), (k1_hbm, k1_ref))
        )
    ]
    for copy in local:
        copy.start()

    has_above, has_left = row > 0, col > 0
    has_below, has_right = row < rows_n - 1, col < cols_n - 1
    senders = (
        (has_below, dict(row=row + 1)),
        (has_right, dict(col=col + 1)),
        (has_below & has_right, dict(row=row + 1, col=col + 1)),
    )
    targets = (
        (has_above, dict(row=row - 1)),
        (has_left, dict(col=col - 1)),
        (has_above & has_left, dict(row=row - 1, col=col - 1)),
    )
    barrier = pltpu.get_barrier_semaphore()
    partners = (
        [dict(row=lax.rem(row + k, rows_n)) for k in range(1, rows_n)]
        + [dict(dp=lax.rem(dp + k, dps)) for k in range(1, dps)]
        + [dict(col=lax.rem(col + k, cols_n)) for k in range(1, cols_n)]
    )
    for change in partners:
        pl.semaphore_signal(barrier, inc=1, device_id=peer(**change), device_id_type=MESH)

    @pl.when(senders[2][0])
    def _():
        pl.semaphore_signal(barrier, inc=1, device_id=peer(**senders[2][1]), device_id_type=MESH)

    local[0].wait()
    local[1].wait()
    su_row[...] = up_ref[0, 0].astype(F32)
    sh_row[...] = hid_ref[0, 0].astype(F32)
    for i in range(ur):
        su_col[i : i + 1] = up_ref[0, i].astype(F32)[0:1]
    for i in range(hr):
        sh_col[i : i + 1] = hid_ref[0, i].astype(F32)[0:1]
    su_cor[...] = up_ref[0, 0].astype(F32)[0:8]
    sh_cor[...] = hid_ref[0, 0].astype(F32)[0:8]
    pl.semaphore_wait(barrier, len(partners) + (has_above & has_left).astype(jnp.int32))

    pairs = (
        ((su_row, u_row), (sh_row, h_row)),
        ((su_col, u_col), (sh_col, h_col)),
        ((su_cor, u_cor), (sh_cor, h_cor)),
    )

    def halo_copies(way, change):
        return [
            pltpu.make_async_remote_copy(
                src_ref=src, dst_ref=dst, send_sem=halo_send.at[2 * way + k],
                recv_sem=halo_recv.at[2 * way + k], device_id=peer(**change), device_id_type=MESH,
            )
            for k, (src, dst) in enumerate(pairs[way])
        ]

    for way, (holds, change) in enumerate(targets):
        @pl.when(holds)
        def _():
            for copy in halo_copies(way, change):
                copy.start()

    uext[0:ur, 0:uc] = up_ref[0].astype(F32)
    for h in range(hw // 128):
        aact[h] = jnp.maximum(hid_ref[0, :, :, h * 128 : (h + 1) * 128].astype(F32), 0.0)
    local[2].wait()
    for h in range(pw // 128):
        pix32[h] = pix_ref[0, :, :, h * 128 : (h + 1) * 128].astype(F32)

    for way, (holds, change) in enumerate(senders):
        @pl.when(holds)
        def _():
            for copy in halo_copies(way, change):
                copy.wait_recv()

        @pl.when(jnp.logical_not(holds))
        def _():
            for _, dst in pairs[way]:
                dst[...] = jnp.zeros(dst.shape, dst.dtype)

    uext[ur, 0:uc] = u_row[...]
    for i in range(ur):
        uext[i, uc : uc + 1] = u_col[i : i + 1]
    uext[ur, uc : uc + 1] = u_cor[0:1]
    for (sr, sc), lane in LANE.items():
        part = uext[sr : sr + ur, sc : sc + uc].reshape(ur * uc, uw).astype(BF16)
        ucat[:, lane * uw : (lane + 1) * uw] = part

    if g_ref.shape[0] > 9 * hw:
        g_ref[9 * hw :] = jnp.zeros((g_ref.shape[0] - 9 * hw, width), BF16)

    started = []

    def send(src, dst, send_sem, recv_sem, change):
        copy = pltpu.make_async_remote_copy(
            src_ref=src, dst_ref=dst, send_sem=send_sem, recv_sem=recv_sem,
            device_id=peer(**change), device_id_type=MESH,
        )
        copy.start()
        started.append(copy)
        return copy

    order = [lax.rem(col + j, cols_n) for j in range(1, cols_n)] + [col]

    def window(r, c):
        return pl.ds(pl.multiple_of((r * cols_n + c) * share // 16 * 16, 16), padded)

    sides = (pl.ds(hw, uw), pl.ds(0, hw))
    copies1 = {}

    def send_rows(side):
        for j, c in enumerate(order):
            for k in range(1, rows_n):
                to = lax.rem(row + k, rows_n)
                copies1[side, k, j] = send(
                    g_ref.at[window(to, c), sides[side]], in1.at[k - 1, j, :, sides[side]],
                    s1.at[side, k - 1, j], r1.at[side, k - 1, j], dict(row=to),
                )

    def parity_rows(ref, pr, pc, rows, cols, wide):
        parts = [
            jnp.stack([ref[h, 2 * k + pr, pl.ds(pc, cols, stride=2), :] for k in range(rows)])
            for h in range(wide // 128)
        ]
        return jnp.concatenate(parts, axis=-1).reshape(rows * cols, wide).astype(BF16)

    for pr, pc in PARITIES:
        act = parity_rows(aact, pr, pc, ur, uc, hw)
        terms = terms_of(pr, pc)
        first = terms[0][0]
        total = dot_0(act, ucat[:, first * uw : (first + len(terms)) * uw]) * scale_two
        for n, (_, a, b, _) in enumerate(terms):
            g_ref[pl.ds((3 * a + b) * hw, hw), sides[0]] = total[:, n * uw : (n + 1) * uw].astype(BF16)
    send_rows(0)

    local[3].wait()
    for pr, pc in PARITIES:
        kr = ur + 1 - pr
        total = None
        for _, a, b, (sr, sc) in terms_of(pr, pc):
            u = uext[sr : sr + kr, sc : sc + ucp].reshape(kr * ucp, uw).astype(BF16)
            term = dot_t(u, k2_ref[a, b])
            total = term if total is None else total + term
        total = total.reshape(kr, ucp, hw)
        for k in range(kr):
            for lo in range(0, hw, 128):
                gext[lo // 128, 2 * k + pr, pl.ds(pc, ucp, stride=2), :] = total[k, :, lo : lo + 128]
    for p in range(hr + 1):
        hid = hid_ref[0, p].astype(F32) if p < hr else h_row[...]
        edge = h_col[p : p + 1] if p < hr else h_cor[0:1]
        for lo in range(0, hw, 128):
            cut = slice(lo, lo + 128)
            eext[p, 0:hc, cut] = jnp.where(hid[:, cut] > 0, gext[lo // 128, p, 0:hc], 0.0)
            eext[p, hc : hc + 1, cut] = jnp.where(
                edge[:, cut] > 0, gext[lo // 128, p, hc : hc + 1], 0.0
            )
    for (sr, sc), lane in LANE.items():
        part = eext[sr : sr + hr, sc : sc + hc].reshape(hr * hc, hw).astype(BF16)
        ecat[:, lane * hw : (lane + 1) * hw] = part

    for pr, pc in PARITIES:
        pix = parity_rows(pix32, pr, pc, hr, hc, pw)
        terms = terms_of(pr, pc)
        first = terms[0][0]
        total = dot_0(pix, ecat[:, first * hw : (first + len(terms)) * hw]) * scale_one
        for n, (_, a, b, _) in enumerate(terms):
            g_ref[pl.ds((3 * a + b) * hw, hw), sides[1]] = total[:, n * hw : (n + 1) * hw].astype(BF16)
    send_rows(1)

    def pixel_gradient(pr, pc):
        total = None
        for lane, a, b, _ in terms_of(pr, pc):
            term = dot_t(ecat[:, lane * hw : (lane + 1) * hw], k1_ref[a, b])
            total = term if total is None else total + term
        total = total.reshape(hr, hc, pw)
        for k in range(hr):
            for h in range(pw // 128):
                pix32[h, 2 * k + pr, pl.ds(pc, hc, stride=2), :] = total[k, :, h * 128 : (h + 1) * 128]

    local[4].wait()
    copies2, copies3, copies4 = {}, {}, {}
    for j, c in enumerate(order):
        for pr, pc in PARITIES[j : j + 1]:
            pixel_gradient(pr, pc)
        for k in range(1, rows_n):
            copies1[0, k, j].wait_recv()
            copies1[1, k, j].wait_recv()
        total = g_ref[window(row, c), :].astype(F32)
        for k in range(1, rows_n):
            total = total + in1[k - 1, j].astype(F32)
        for y in range(2):
            for x in range(2):
                acc1[j, y, x] = total[y * half : (y + 1) * half, x * lanes : (x + 1) * lanes].astype(BF16)
        for k in range(1, dps):
            to = lax.rem(dp + k, dps)
            copies2[k, j] = send(
                acc1.at[j, to // 2, to % 2], in2.at[k - 1, j], s2.at[k - 1, j], r2.at[k - 1, j],
                dict(dp=to),
            )
    for pr, pc in PARITIES[cols_n:]:
        pixel_gradient(pr, pc)
    for h in range(pw // 128):
        out_ref[0, :, :, h * 128 : (h + 1) * 128] = pix32[h].astype(BF16)
    out_copy = pltpu.make_async_copy(out_ref, out_hbm, local_sem.at[5])
    out_copy.start()

    for j, c in enumerate(order):
        total = acc1[j, dp // 2, dp % 2].astype(F32)
        for k in range(1, dps):
            copies2[k, j].wait_recv()
            total = total + in2[k - 1, j].astype(F32)
        if j < cols_n - 1:
            acc2[j] = total.astype(BF16)
            copies3[j] = send(acc2.at[j], in3.at[j], s3.at[j], r3.at[j], dict(col=c))
    for j in range(cols_n - 1):
        copies3[j].wait_recv()
        total = total + in3[j].astype(F32)
    mine[...] = total.astype(BF16)
    for k in range(1, dps):
        to = lax.rem(dp + k, dps)
        copies4[k] = send(mine, in4.at[dp // 2, dp % 2], s4.at[k - 1], r4.at[k - 1], dict(dp=to))
    in4[dp // 2, dp % 2] = mine[...]
    for k in range(1, dps):
        copies4[k].wait_recv()
    for y in range(2):
        whole = jnp.concatenate([in4[y, 0], in4[y, 1]], axis=-1).astype(F32)
        g1_out[y * half : (y + 1) * half] = whole[:, 0:hw]
        g2_out[y * half : (y + 1) * half] = whole[:, hw:]
    out_copy.wait()
    for copy in started:
        copy.wait_send()
    for way, (holds, change) in enumerate(targets):
        @pl.when(holds)
        def _():
            for copy in halo_copies(way, change):
                copy.wait_send()


def fused(pixels, hidden, upstream, kernel_first, kernel_second, mesh):
    dps, rows_n, cols_n = (mesh.shape[name] for name in NAMES)
    _, ur, uc, uw = upstream.shape
    _, hr, hc, hw = hidden.shape
    _, pr, pc, pw = pixels.shape
    scale_one = 1.0 / math.sqrt(mesh.size * hr * hc)
    scale_two = 1.0 / math.sqrt(mesh.size * ur * uc)
    ucp = (uc // 8 + 1) * 8
    share = 9 * hw // (rows_n * cols_n)
    exact = share % 32 == 0
    padded = share if exact else -(-(share + 15) // 32) * 32
    g_rows = 9 * hw + (0 if exact else padded)
    width = hw + uw
    half, lanes = padded // 2, width // 2
    halo = [(uc, uw), (ur, uw), (8, uw), (hc, hw), (hr, hw), (8, hw)]
    dma = pltpu.SemaphoreType.DMA
    anywhere = pl.BlockSpec(memory_space=pl.ANY)
    vmem = pl.BlockSpec(memory_space=pltpu.VMEM)
    grad_pixels, g1, g2 = pl.pallas_call(
        functools.partial(
            fused_kernel, dps, rows_n, cols_n, share, padded, scale_one, scale_two
        ),
        out_shape=[
            jax.ShapeDtypeStruct(pixels.shape, BF16),
            jax.ShapeDtypeStruct((padded, hw), F32),
            jax.ShapeDtypeStruct((padded, uw), F32),
        ],
        in_specs=[anywhere] * 5,
        out_specs=[anywhere, vmem, vmem],
        scratch_shapes=[
            pltpu.VMEM(a.shape, BF16)
            for a in (pixels, hidden, upstream, kernel_first, kernel_second, pixels)
        ]
        + [pltpu.VMEM(s, F32) for s in halo + halo]
        + [
            pltpu.VMEM((ur + 2, ucp + 8, uw), F32),
            pltpu.VMEM((hw // 128, hr + 2, 2 * ucp, 128), F32),
            pltpu.VMEM((hr + 1, hc + 8, hw), F32),
            pltpu.VMEM((ur * uc, 4 * uw), BF16),
            pltpu.VMEM((hr * hc, 4 * hw), BF16),
            pltpu.VMEM((hw // 128, hr, hc, 128), F32),
            pltpu.VMEM((pw // 128, pr, pc, 128), F32),
            pltpu.VMEM((g_rows, width), BF16),
            pltpu.VMEM((cols_n, 2, 2, half, lanes), BF16),
            pltpu.VMEM((rows_n - 1, cols_n, padded, width), BF16),
            pltpu.VMEM((cols_n - 1, half, lanes), BF16),
            pltpu.VMEM((dps - 1, cols_n, half, lanes), BF16),
            pltpu.VMEM((cols_n - 1, half, lanes), BF16),
            pltpu.VMEM((half, lanes), BF16),
            pltpu.VMEM((2, 2, half, lanes), BF16),
            dma((6,)), dma((6,)), dma((6,)),
            dma((2, rows_n - 1, cols_n)), dma((2, rows_n - 1, cols_n)),
            dma((dps - 1, cols_n)), dma((dps - 1, cols_n)),
            dma((cols_n - 1,)), dma((cols_n - 1,)),
            dma((dps - 1,)), dma((dps - 1,)),
        ],
        compiler_params=pltpu.CompilerParams(
            collective_id=0, has_side_effects=True, vmem_limit_bytes=56 * 2**20
        ),
    )(pixels, hidden, upstream, kernel_first, kernel_second)
    if not exact:
        at = (lax.axis_index("row") * cols_n + lax.axis_index("col")) * share % 16
        g1, g2 = (lax.dynamic_slice_in_dim(g, at, share, 0) for g in (g1, g2))
    return grad_pixels, g1, g2


def solution(mesh):
    def per_device(*args):
        return tuple(fused(*args, mesh))

    in_specs = (P("dp", "row", "col", None),) * 3 + (P(), P())
    out_specs = (P("dp", "row", "col", None), P(("row", "col"), None), P(("row", "col"), None))
    return jax.shard_map(
        per_device, mesh=mesh, in_specs=in_specs, out_specs=out_specs, check_vma=False
    )
```

time: 335 us -> 47.5 us (0.14)
  waiting for transfers between devices: 168 us -> 0 us
  local copies, waits for them, and re-layouts: 94.8 us -> 4.26 us
  Pallas kernels: 0 us -> 42.4 us
  starting transfers between devices: 27.9 us -> 0 us
  other arithmetic: 16.2 us -> 0 us
  between operations: 14.4 us -> 0.66 us
  matrix products: 10.6 us -> 0 us
    reduce_scatter x2 -> x0, waiting for transfers between devices: 119 us -> none  [kernel_gradient(): lax.psum_scatter(slide_sums, ('row', 'col'), scatter_dimension=0, tiled=T...]
    slice x28 -> x0, local copies, waits for them, and re-layouts: 58.3 us -> none  [the longest x18 53.5 us: gather_taps(): extended[tap_row:tap_row + 2 * out_rows:2, tap_col:tap_col + 2 * out_cols:2]]
    psum x1 -> x0, waiting for transfers between devices: 45.9 us -> none  [kernel_gradient(): lax.psum(lax.dot_general(patches, gradient, (((0,), (0,)), ((), ())), pre...]
    pallas_call x0 -> x1, Pallas kernels: none -> 42.4 us  [fused(): pl.pallas_call(functools.partial(fused_kernel, dps, rows_n, cols_n, share...]
    ppermute x12 -> x0, starting transfers between devices: 27.6 us -> none  [shifted(): return lax.ppermute(value, axis, pairs)]
    unnamed x44 -> x7, local copies, waits for them, and re-layouts: 16.4 us -> 4.26 us
    dot_general x4 -> x0, matrix products: 10.6 us -> none  [the longest x2 7.61 us: kernel_gradient(): lax.dot_general(patches, gradient, (((0,), (0,)), ((), ())), preferred_el...]
    another operation x9 -> x0, local copies, waits for them, and re-layouts: 6.13 us -> none  [the longest x4 5.18 us: spread_taps(): jnp.stack([even_part, odd_part], axis=2)]
  transfers between devices with their start and end apart: 15 -> 0, of which waited for: 4 -> 0; matrix products, arithmetic and copies ran while one was open for 28% -> 0% of each run, Pallas kernels for 0% -> 0%
where the time goes in v3:
time: 47.5 us; the launch traced here: 47.4 us
  Pallas kernels  42.4 us (89%)
  local copies, waits for them, and re-layouts  4.26 us (9%)
  between operations  0.66 us (1%)
    pallas_call x1, Pallas kernels, fused(): pl.pallas_call(functools.partial(fused_kernel, dps, rows_n, cols_n, share...  42.4 us
    unnamed x7, local copies, waits for them, and re-layouts  4.26 us

profile of v3, /device:TPU:0, one launch (start us, length us, event | category | flops | bytes accessed | tf_op | source)
XLA Modules:
  0.0 47.4 jit_solution(10388238642151832234)
XLA Ops:
  0.6 42.4 %shard_map.76 = (bf16[1,32,96,256]{3,2,1,0:T(8,128)(2,1)}, f32[288,256]{1,0:T(8,128)}, f32[288,512]{1,0:T(8,128)}) custom-call(bf16[1,32,96,256]{3,2,1,0:T(8,128)(2,1)} %pix_hbm.1, bf16[1,16,48,256]{3,2,1,0:T(8,128)(2,1)} %hid_hbm.1, bf16[1,8,24,512]{3,2,1,0:T(8,128)(2,1)} %up_hbm.1, bf16[3,3,256,256]{3,2,1,0:T(8,128)(2,1)} %k1_hbm.1, ...), custom_call_target="tpu_custom_call" | custom-call | tf_op jit(solution)/shard_map/pallas_call | solution.py:322
  43.1 0.0 copy-start.1
  43.1 0.0 copy-start
  43.1 2.7 %copy.11 = bf16[1,32,96,256]{3,2,1,0:T(8,128)(2,1)} copy(bf16[1,32,96,256]{3,2,1,0:T(8,128)(2,1)} %get-tuple-element.6) | data formatting | bytes 3145728
  45.8 0.0 copy-done.1
  45.8 0.7 %copy.12 = f32[288,256]{1,0:T(8,128)} copy(f32[288,256]{1,0:T(8,128)S(1)} %copy-done.1) | data formatting | bytes 589824
  46.5 0.0 copy-done
  46.5 0.8 %copy.13 = f32[288,512]{1,0:T(8,128)} copy(f32[288,512]{1,0:T(8,128)S(1)} %copy-done) | data formatting | bytes 1179648
Async XLA Ops:
  43.1 2.8 %copy-start.1 = (f32[288,256]{1,0:T(8,128)S(1)}, f32[288,256]{1,0:T(8,128)}, u32[]{:S(2)}) copy-start(f32[288,256]{1,0:T(8,128)} %get-tuple-element.7) | copy-start | bytes 884740
  43.1 3.5 %copy-start = (f32[288,512]{1,0:T(8,128)S(1)}, f32[288,512]{1,0:T(8,128)}, u32[]{:S(2)}) copy-start(f32[288,512]{1,0:T(8,128)} %get-tuple-element.8) | copy-start | bytes 1769476

commit v4 on v3

--- a/solution.py
+++ b/solution.py
@@ -223,6 +223,30 @@
         part = eext[sr : sr + hr, sc : sc + hc].reshape(hr * hc, hw).astype(BF16)
         ecat[:, lane * hw : (lane + 1) * hw] = part
 
+    parts = (pl.ds(0, uw // 2), pl.ds(uw // 2, hw // 2))
+    copies2 = {}
+
+    def row_sums(side, j):
+        total = g_ref[window(row, order[j]), sides[side]].astype(F32)
+        for k in range(1, rows_n):
+            copies1[side, k, j].wait_recv()
+            total = total + in1[k - 1, j, :, sides[side]].astype(F32)
+        wide = total.shape[-1] // 2
+        for y in range(2):
+            for x in range(2):
+                acc1[j, y, x, :, parts[side]] = total[
+                    y * half : (y + 1) * half, x * wide : (x + 1) * wide
+                ].astype(BF16)
+        for k in range(1, dps):
+            to = lax.rem(dp + k, dps)
+            copies2[side, k, j] = send(
+                acc1.at[j, to // 2, to % 2, :, parts[side]], in2.at[k - 1, j, :, parts[side]],
+                s2.at[side, k - 1, j], r2.at[side, k - 1, j], dict(dp=to),
+            )
+
+    for j in range(cols_n):
+        row_sums(0, j)
+
     for pr, pc in PARITIES:
         pix = parity_rows(pix32, pr, pc, hr, hc, pw)
         terms = terms_of(pr, pc)
@@ -243,25 +267,11 @@
                 pix32[h, 2 * k + pr, pl.ds(pc, hc, stride=2), :] = total[k, :, h * 128 : (h + 1) * 128]
 
     local[4].wait()
-    copies2, copies3, copies4 = {}, {}, {}
+    copies3, copies4 = {}, {}
     for j, c in enumerate(order):
         for pr, pc in PARITIES[j : j + 1]:
             pixel_gradient(pr, pc)
-        for k in range(1, rows_n):
-            copies1[0, k, j].wait_recv()
-            copies1[1, k, j].wait_recv()
-        total = g_ref[window(row, c), :].astype(F32)
-        for k in range(1, rows_n):
-            total = total + in1[k - 1, j].astype(F32)
-        for y in range(2):
-            for x in range(2):
-                acc1[j, y, x] = total[y * half : (y + 1) * half, x * lanes : (x + 1) * lanes].astype(BF16)
-        for k in range(1, dps):
-            to = lax.rem(dp + k, dps)
-            copies2[k, j] = send(
-                acc1.at[j, to // 2, to % 2], in2.at[k - 1, j], s2.at[k - 1, j], r2.at[k - 1, j],
-                dict(dp=to),
-            )
+        row_sums(1, j)
     for pr, pc in PARITIES[cols_n:]:
         pixel_gradient(pr, pc)
     for h in range(pw // 128):
@@ -272,7 +282,8 @@
     for j, c in enumerate(order):
         total = acc1[j, dp // 2, dp % 2].astype(F32)
         for k in range(1, dps):
-            copies2[k, j].wait_recv()
+            copies2[0, k, j].wait_recv()
+            copies2[1, k, j].wait_recv()
             total = total + in2[k - 1, j].astype(F32)
         if j < cols_n - 1:
             acc2[j] = total.astype(BF16)
@@ -288,9 +299,9 @@
     for k in range(1, dps):
         copies4[k].wait_recv()
     for y in range(2):
-        whole = jnp.concatenate([in4[y, 0], in4[y, 1]], axis=-1).astype(F32)
-        g1_out[y * half : (y + 1) * half] = whole[:, 0:hw]
-        g2_out[y * half : (y + 1) * half] = whole[:, hw:]
+        for side, out in enumerate((g2_out, g1_out)):
+            both = [in4[y, x, :, parts[side]] for x in range(2)]
+            out[y * half : (y + 1) * half] = jnp.concatenate(both, axis=-1).astype(F32)
     out_copy.wait()
     for copy in started:
         copy.wait_send()
@@ -353,7 +364,7 @@
             pltpu.VMEM((2, 2, half, lanes), BF16),
             dma((6,)), dma((6,)), dma((6,)),
             dma((2, rows_n - 1, cols_n)), dma((2, rows_n - 1, cols_n)),
-            dma((dps - 1, cols_n)), dma((dps - 1, cols_n)),
+            dma((2, dps - 1, cols_n)), dma((2, dps - 1, cols_n)),
             dma((cols_n - 1,)), dma((cols_n - 1,)),
             dma((dps - 1,)), dma((dps - 1,)),
         ],

time: 47.5 us -> 49.4 us (1.040)
  Pallas kernels: 42.4 us -> 44.3 us
    pallas_call x1, Pallas kernels: 42.4 us -> 44.3 us  [fused(): pl.pallas_call(functools.partial(fused_kernel, dps, rows_n, cols_n, share...]
where the time goes in v4:
time: 49.4 us; the launch traced here: 49.2 us
  Pallas kernels  44.3 us (90%)
  local copies, waits for them, and re-layouts  4.26 us (9%)
  between operations  0.66 us (1%)
    pallas_call x1, Pallas kernels, fused(): pl.pallas_call(functools.partial(fused_kernel, dps, rows_n, cols_n, share...  44.3 us
    unnamed x7, local copies, waits for them, and re-layouts  4.26 us

profile of v4, /device:TPU:0, one launch (start us, length us, event | category | flops | bytes accessed | tf_op | source)
XLA Modules:
  0.0 49.2 jit_solution(6653179137297055040)
XLA Ops:
  0.6 44.3 %shard_map.76 = (bf16[1,32,96,256]{3,2,1,0:T(8,128)(2,1)}, f32[288,256]{1,0:T(8,128)}, f32[288,512]{1,0:T(8,128)}) custom-call(bf16[1,32,96,256]{3,2,1,0:T(8,128)(2,1)} %pix_hbm.1, bf16[1,16,48,256]{3,2,1,0:T(8,128)(2,1)} %hid_hbm.1, bf16[1,8,24,512]{3,2,1,0:T(8,128)(2,1)} %up_hbm.1, bf16[3,3,256,256]{3,2,1,0:T(8,128)(2,1)} %k1_hbm.1, ...), custom_call_target="tpu_custom_call" | custom-call | tf_op jit(solution)/shard_map/pallas_call | solution.py:333
  45.0 0.0 copy-start.1
  45.0 0.0 copy-start
  45.0 2.7 %copy.11 = bf16[1,32,96,256]{3,2,1,0:T(8,128)(2,1)} copy(bf16[1,32,96,256]{3,2,1,0:T(8,128)(2,1)} %get-tuple-element.6) | data formatting | bytes 3145728
  47.7 0.0 copy-done.1
  47.7 0.7 %copy.12 = f32[288,256]{1,0:T(8,128)} copy(f32[288,256]{1,0:T(8,128)S(1)} %copy-done.1) | data formatting | bytes 589824
  48.4 0.0 copy-done
  48.4 0.8 %copy.13 = f32[288,512]{1,0:T(8,128)} copy(f32[288,512]{1,0:T(8,128)S(1)} %copy-done) | data formatting | bytes 1179648
Async XLA Ops:
  45.0 2.8 %copy-start.1 = (f32[288,256]{1,0:T(8,128)S(1)}, f32[288,256]{1,0:T(8,128)}, u32[]{:S(2)}) copy-start(f32[288,256]{1,0:T(8,128)} %get-tuple-element.7) | copy-start | bytes 884740
  45.0 3.5 %copy-start = (f32[288,512]{1,0:T(8,128)S(1)}, f32[288,512]{1,0:T(8,128)}, u32[]{:S(2)}) copy-start(f32[288,512]{1,0:T(8,128)} %get-tuple-element.8) | copy-start | bytes 1769476
